TPU v7x, 32 devices: a whole 2x2x4 slice. The times are simulated.
32 devices in a mesh: row: 4 (over y, core), col: 8 (over z, x).
Axes of the slice: x: 2, y: 2, z: 4, core: 2. Of those that a mesh axis runs over, the one named last changes fastest.
Arguments:
- fields: float32 [4096, 5, 4096], P(('row', 'col')), as said below
- counts: int32 [4, 8], P('row', 'col'), may hold values from 1 to 128, 512 in all within a row
Outputs:
- fields_out: float32 [4096, 5, 4096], P(('row', 'col'))
Inputs may be any that keep to these rules, and one draw needn't show every extreme that they name: `fields`: in every slot, also those that hold no patch, density lies in 0.5 to 3, pressure 0.4 (E - |m|^2 / (2 rho)) in 0.5 to 2 and each velocity component in -0.5 to 0.5. Each index of row holds 512 patches in all: the entries of counts[r] sum to 512, and some device of each index of row holds 128.
All inputs are finite; a program needn't handle non-finite values.
Results may differ from a plain program's by a relative error of at most 0.0003.
Values sent between devices are 32-bit elements; how exact they have to be, the bound alone decides.
A program may use at most 192 MiB of HBM per device.

v0:
```python
import math

import jax
import jax.numpy as jnp
from jax import lax
from jax.sharding import PartitionSpec as P

PE = 16
GX = 256
GY = 256
GZ = 128


gamma_gas = 1.4
speed_bound = 4.0
time_step = 0.03
four_pi_g = 10.0


def padded(block, sides, width):
    for axis, dim in sides:
        count = lax.axis_size(axis)
        forward = [(i, i + 1) for i in range(count - 1)]
        forward.append((count - 1, 0))
        backward = [(target, source) for source, target in forward]
        low = lax.ppermute(
            lax.slice_in_dim(block, block.shape[dim] - width, None, axis=dim), axis, forward
        )
        high = lax.ppermute(lax.slice_in_dim(block, 0, width, axis=dim), axis, backward)
        block = jnp.concatenate([low, block, high], axis=dim)
    return block


def minmod_slope(lower_gap, upper_gap):
    return (
        0.5
        * (jnp.sign(lower_gap) + jnp.sign(upper_gap))
        * jnp.minimum(jnp.abs(lower_gap), jnp.abs(upper_gap))
    )


def normal_flux(states, direction):
    density = states[0]
    momenta = states[1:4]
    energy = states[4]
    velocity = momenta[direction] / density
    kinetic = (
        0.5
        * (momenta[0] * momenta[0] + momenta[1] * momenta[1] + momenta[2] * momenta[2])
        / density
    )
    pressure = (gamma_gas - 1.0) * (energy - kinetic)
    pieces = [momenta[direction]]
    for component in range(3):
        flux_term = momenta[component] * velocity
        if component == direction:
            flux_term = flux_term + pressure
        pieces.append(flux_term)
    pieces.append((energy + pressure) * velocity)
    return jnp.stack(pieces)


def cut_range(array, dim_index, first_cell, count_cells):
    return lax.slice_in_dim(array, first_cell, first_cell + count_cells, axis=dim_index)


def face_rates(states):
    total_rate = None
    for direction in range(3):
        dim_index = direction + 1
        trimmed = states
        for other_dim in (1, 2):
            if other_dim != dim_index:
                trimmed = cut_range(trimmed, other_dim, 2, trimmed.shape[other_dim] - 4)
        if direction < 2:
            length = trimmed.shape[dim_index]
            lower_cell = cut_range(trimmed, dim_index, 0, length - 3)
            centre = cut_range(trimmed, dim_index, 1, length - 3)
            upper_cell = cut_range(trimmed, dim_index, 2, length - 3)
            far_cell = cut_range(trimmed, dim_index, 3, length - 3)
        else:
            lower_cell = jnp.roll(trimmed, 1, 3)
            centre = trimmed
            upper_cell = jnp.roll(trimmed, -1, 3)
            far_cell = jnp.roll(trimmed, -2, 3)
        left_state = centre + 0.5 * minmod_slope(centre - lower_cell, upper_cell - centre)
        right_state = upper_cell - 0.5 * minmod_slope(upper_cell - centre, far_cell - upper_cell)
        face_flux = 0.5 * (
            normal_flux(left_state, direction) + normal_flux(right_state, direction)
        ) - 0.5 * speed_bound * (right_state - left_state)
        if direction < 2:
            change = cut_range(face_flux, dim_index, 1, length - 4) - cut_range(
                face_flux, dim_index, 0, length - 4
            )
        else:
            change = face_flux - jnp.roll(face_flux, 1, 3)
        total_rate = change if total_rate is None else total_rate + change
    return -total_rate


def crop_plane(array, margin):
    return array[:, margin : array.shape[1] - margin, margin : array.shape[2] - margin, :]


def advance(extended):
    first = crop_plane(extended, 2) + time_step * face_rates(extended)
    second = crop_plane(first, 2) + time_step * face_rates(first)
    return 0.5 * crop_plane(extended, 4) + 0.5 * second


def lap_eigen(wave, length):
    return 2.0 * jnp.cos(2.0 * math.pi / length * wave) - 2.0


def apply_kick(stepped, gradient):
    density = stepped[0]
    momenta = stepped[1:4]
    new_momenta = momenta - time_step * density[None] * gradient
    work_done = momenta[0] * gradient[0] + momenta[1] * gradient[1] + momenta[2] * gradient[2]
    new_energy = stepped[4] - time_step * work_done
    return jnp.concatenate([stepped[0:1], new_momenta, new_energy[None]], axis=0)


def dft_tables(length):
    indices = jnp.arange(length, dtype=jnp.int32)
    wrapped = indices[:, None] * indices[None, :] % length
    angles = 2.0 * math.pi / length * wrapped.astype(jnp.float32)
    return (jnp.cos(angles), jnp.sin(angles))


def right_mul(values, matrix):
    return jnp.matmul(values, matrix, precision=lax.Precision.HIGHEST)


def left_mul(matrix, values):
    return jnp.einsum("yk,...km->...ym", matrix, values, precision=lax.Precision.HIGHEST)


def on_device(fields, counts):
    rows_count = lax.axis_size("row")
    cols_count = lax.axis_size("col")
    my_row = lax.axis_index("row")
    my_column = lax.axis_index("col")
    capacity = fields.shape[0]
    block_x = GX // rows_count
    block_y = GY // cols_count
    lat_x = block_x // PE
    lat_y = GY // PE
    lat_z = GZ // PE
    brick_y = min(PE, block_y)
    per_patch = PE // brick_y
    per_pencil_y = block_y // brick_y
    repeat_y = max(1, block_y // PE)
    per_peer = (capacity + lat_y - 1) // lat_y * repeat_y
    brick_cells = 5 * PE * brick_y * PE
    buffer_rows = cols_count * per_peer
    row_counts = lax.all_gather(counts, "col", axis=1, tiled=True).reshape(cols_count)
    starts = jnp.cumsum(row_counts) - row_counts
    column_ids = jnp.arange(cols_count, dtype=jnp.int32)
    own_start = jnp.sum(jnp.where(column_ids == my_column, starts, 0))
    own_count = counts[0, 0]
    slot_ids = jnp.arange(capacity, dtype=jnp.int32)
    brick_ids = jnp.arange(per_patch, dtype=jnp.int32)
    y_patch = (own_start + slot_ids) % lat_y
    global_y = y_patch[:, None] * PE + brick_ids[None, :] * brick_y
    slot_inner = (slot_ids // lat_y * repeat_y + y_patch % repeat_y)[:, None]
    dest_index = (global_y // block_y * per_peer + slot_inner).reshape(-1)
    live_slots = jnp.broadcast_to((slot_ids < own_count)[:, None], (capacity, per_patch)).reshape(
        -1
    )
    buffer_ids = jnp.arange(buffer_rows, dtype=jnp.int32)
    send_select = ((buffer_ids[:, None] == dest_index[None, :]) & live_slots[None, :]).astype(
        jnp.float32
    )
    grid_xl = jnp.arange(lat_x, dtype=jnp.int32)[:, None, None]
    grid_w = jnp.arange(per_pencil_y, dtype=jnp.int32)[None, :, None]
    grid_zl = jnp.arange(lat_z, dtype=jnp.int32)[None, None, :]
    pencil_y = (my_column * block_y + grid_w * brick_y) // PE
    curve_pos = (grid_xl * lat_z + grid_zl) * lat_y + pencil_y
    curve_pos = curve_pos.reshape(-1)
    y_flat = jnp.broadcast_to(pencil_y, (lat_x, per_pencil_y, lat_z)).reshape(-1)
    owner = jnp.sum((starts[None, :] <= curve_pos[:, None]).astype(jnp.int32), axis=1) - 1
    owner_start = jnp.sum(
        jnp.where(column_ids[None, :] == owner[:, None], starts[None, :], 0), axis=1
    )
    source_index = (
        owner * per_peer + (curve_pos - owner_start) // lat_y * repeat_y + y_flat % repeat_y
    )
    recv_select = (buffer_ids[None, :] == source_index[:, None]).astype(jnp.float32)
    patch_bricks = (
        fields.reshape(capacity, 5, PE, per_patch, brick_y, PE)
        .transpose(0, 3, 1, 2, 4, 5)
        .reshape(capacity * per_patch, brick_cells)
    )
    send_buffer = jnp.matmul(send_select, patch_bricks, precision=lax.Precision.HIGHEST)
    arrived = lax.all_to_all(send_buffer, "col", split_axis=0, concat_axis=0, tiled=True)
    pencil_bricks = jnp.matmul(recv_select, arrived, precision=lax.Precision.HIGHEST)
    pencil = (
        pencil_bricks.reshape(lat_x, per_pencil_y, lat_z, 5, PE, brick_y, PE)
        .transpose(3, 0, 4, 1, 5, 2, 6)
        .reshape(5, block_x, block_y, GZ)
    )
    extended = padded(pencil, (("row", 1), ("col", 2)), 4)
    stepped = advance(extended)
    rows_y = GY // rows_count
    cols_z = GZ // cols_count
    cos_x, sin_x = dft_tables(GX)
    cos_y, sin_y = dft_tables(GY)
    cos_z, sin_z = dft_tables(GZ)
    density = stepped[0]
    along_re = right_mul(density, cos_z)
    along_im = -right_mul(density, sin_z)
    packed = (
        jnp.stack([along_re, along_im])
        .reshape(2, block_x, block_y, cols_count, cols_z)
        .transpose(3, 2, 0, 4, 1)
    )
    paired = lax.all_to_all(packed, "col", split_axis=0, concat_axis=0, tiled=True)
    paired = paired.reshape(GY, 2, cols_z * block_x)
    mid_re = paired[:, 0]
    mid_im = paired[:, 1]
    spec_re = left_mul(cos_y, mid_re) + left_mul(sin_y, mid_im)
    spec_im = left_mul(cos_y, mid_im) - left_mul(sin_y, mid_re)
    packed = (
        jnp.stack([spec_re, spec_im])
        .reshape(2, rows_count, rows_y, cols_z * block_x)
        .transpose(1, 0, 2, 3)
    )
    paired = lax.all_to_all(packed, "row", split_axis=0, concat_axis=0, tiled=True)
    paired = (
        paired.reshape(rows_count, 2, rows_y, cols_z, block_x)
        .transpose(1, 2, 3, 0, 4)
        .reshape(2, rows_y * cols_z, GX)
    )
    spec_re = right_mul(paired[0], cos_x) + right_mul(paired[1], sin_x)
    spec_im = right_mul(paired[1], cos_x) - right_mul(paired[0], sin_x)
    index_x = jnp.arange(GX, dtype=jnp.int32)
    index_y = my_row * rows_y + jnp.arange(rows_y, dtype=jnp.int32)
    index_z = my_column * cols_z + jnp.arange(cols_z, dtype=jnp.int32)
    wave_x = index_x.astype(jnp.float32)
    wave_y = index_y.astype(jnp.float32)
    wave_z = index_z.astype(jnp.float32)
    eigen = (
        lap_eigen(wave_x, GX)[None, None, :]
        + lap_eigen(wave_y, GY)[:, None, None]
        + lap_eigen(wave_z, GZ)[None, :, None]
    )
    zero_mode = (
        (index_x == 0)[None, None, :]
        & (index_y == 0)[:, None, None]
        & (index_z == 0)[None, :, None]
    )
    green = jnp.where(zero_mode, 0.0, four_pi_g / jnp.where(zero_mode, -1.0, eigen)).reshape(
        rows_y * cols_z, GX
    )
    pot_re = spec_re * green
    pot_im = spec_im * green
    scale = 1.0 / (GX * GY * GZ)
    sine_x = jnp.sin(2.0 * math.pi / GX * wave_x)[None, :]
    sine_y = jnp.broadcast_to(
        jnp.sin(2.0 * math.pi / GY * wave_y)[:, None], (rows_y, cols_z)
    ).reshape(rows_y * cols_z, 1)
    sine_z = jnp.broadcast_to(
        jnp.sin(2.0 * math.pi / GZ * wave_z)[None, :], (rows_y, cols_z)
    ).reshape(rows_y * cols_z, 1)
    grad_re = jnp.stack([-(sine_x * pot_im), -(sine_y * pot_im), -(sine_z * pot_im)])
    grad_im = jnp.stack([sine_x * pot_re, sine_y * pot_re, sine_z * pot_re])
    back_re = right_mul(grad_re, cos_x) - right_mul(grad_im, sin_x)
    back_im = right_mul(grad_im, cos_x) + right_mul(grad_re, sin_x)
    packed = (
        jnp.stack([back_re, back_im], axis=1)
        .reshape(3, 2, rows_y, cols_z, rows_count, block_x)
        .transpose(4, 0, 1, 2, 3, 5)
    )
    returned = lax.all_to_all(packed, "row", split_axis=0, concat_axis=0, tiled=True)
    returned = returned.transpose(1, 2, 0, 3, 4, 5).reshape(3, 2, GY, cols_z * block_x)
    mid_re = left_mul(cos_y, returned[:, 0]) - left_mul(sin_y, returned[:, 1])
    mid_im = left_mul(cos_y, returned[:, 1]) + left_mul(sin_y, returned[:, 0])
    packed = (
        jnp.stack([mid_re, mid_im], axis=1)
        .reshape(3, 2, cols_count, block_y, cols_z * block_x)
        .transpose(2, 0, 1, 3, 4)
    )
    returned = lax.all_to_all(packed, "col", split_axis=0, concat_axis=0, tiled=True)
    returned = (
        returned.reshape(cols_count, 3, 2, block_y, cols_z, block_x)
        .transpose(1, 2, 5, 3, 0, 4)
        .reshape(3, 2, block_x, block_y, GZ)
    )
    gradient = (right_mul(returned[:, 0], cos_z) - right_mul(returned[:, 1], sin_z)) * scale
    kicked = apply_kick(stepped, gradient)
    back_bricks = (
        kicked.reshape(5, lat_x, PE, per_pencil_y, brick_y, lat_z, PE)
        .transpose(1, 3, 5, 0, 2, 4, 6)
        .reshape(lat_x * per_pencil_y * lat_z, brick_cells)
    )
    return_buffer = jnp.matmul(recv_select.T, back_bricks, precision=lax.Precision.HIGHEST)
    came_back = lax.all_to_all(return_buffer, "col", split_axis=0, concat_axis=0, tiled=True)
    slot_bricks = jnp.matmul(send_select.T, came_back, precision=lax.Precision.HIGHEST)
    return (
        slot_bricks.reshape(capacity, per_patch, 5, PE, brick_y, PE)
        .transpose(0, 2, 3, 1, 4, 5)
        .reshape(capacity, 5, PE * PE * PE)
    )


def solution(mesh):
    return jax.shard_map(
        on_device,
        mesh=mesh,
        in_specs=(P(("row", "col"), None, None), P("row", "col")),
        out_specs=P(("row", "col"), None, None),
        check_vma=False,
    )
```

profile of v0, /device:TPU:0, one launch (start us, length us, event | category | flops | bytes accessed | tf_op | source)
XLA Modules:
  0.0 1925.0 jit_solution(3134245284968151882)
XLA Ops:
  2.6 13.1 all-reduce
  28.4 11.8 fusion.99
  46.7 224.0 %all-to-all-done = f32[8,16,20480]{2,1,0:T(8,128)} async-done(((f32[8,16,20480]{2,1,0:T(8,128)}), f32[8,16,20480]{2,1,0:T(8,128)}, u32[]{:S(2)}, u32[]{:S(2)}) %all-to-all-start) | async-done | bytes 10485792 | tf_op jit(solution)/shard_map/all_to_all | solution.py:196
  282.4 155.3 %convolution_bitcast_fusion = f32[5,4,16,2,16,8,16]{6,5,4,2,0,3,1:T(8,128)} fusion(f32[5,16,16,16,128,1,1]{4,3,2,1,0,6,5:T(8,128)} %bitcast.239, s32[4,2,8]{2,1,0:T(2,128)S(1)} %fusion.118), kind=kOutput, calls=%fused_computation.1 | convolution fusion | flops 2013274112 | bytes 15728896 | tf_op jit(solution)/shard_map/dot_general | solution.py:197
  437.7 28.8 %copy.61 = f32[5,4,16,2,16,8,16]{6,5,4,3,2,1,0:T(8,128)} copy(f32[5,4,16,2,16,8,16]{6,5,4,2,0,3,1:T(8,128)} %convolution_bitcast_fusion) | data formatting | bytes 10485760 | tf_op jit(solution)/shard_map/transpose | solution.py:200
  466.5 26.5 %reshape.525 = f32[5,64,32,128]{3,2,1,0:T(8,128)} reshape(f32[5,4,16,2,16,8,16]{6,5,4,3,2,1,0:T(8,128)} %copy.61) | data formatting | bytes 10485760 | tf_op jit(solution)/shard_map/reshape | solution.py:201
  514.0 27.7 %collective-permute-done.2 = f32[5,72,4,128]{3,2,1,0:T(4,128)S(1)} collective-permute-done((f32[5,72,4,128]{3,2,1,0:T(4,128)S(1)}, f32[5,72,4,128]{3,2,1,0:T(4,128)S(1)}, u32[]{:S(2)}, u32[]{:S(2)}) %collective-permute-start.2) | collective-permute-done | bytes 737312 | tf_op jit(solution)/shard_map/ppermute | solution.py:26
  549.3 12.1 fusion.217
  561.4 12.1 fusion.218
  584.8 13.4 multiply_add_fusion
  598.2 12.8 multiply_add_fusion.2
  611.1 21.7 %multiply_add_fusion.1 = (f32[5,68,36,128]{3,2,1,0:T(8,128)S(1)}, f32[5,68,36,128]{3,2,1,0:T(8,128)}) fusion(f32[5,68,36,127]{3,2,1,0:T(8,128)} %get-tuple-element.57, f32[5,68,36,1]{3,2,1,0:T(8,128)} %get-tuple-element.55, f32[5,72,40,128]{3,2,1,0:T(8,128)S(1)} %copy-done, f32[5,68,36,1]{3,2,1,0:T(8,128)} %get-tuple-element.56, ...), kind=kLoop, calls=%fused_computation.25 | loop fusion | flops 37601280 | bytes 37601280 | tf_op jit(solution)/shard_map/add | solution.py:86
  717.2 22.0 %fusion.4 = f32[5,68,36,128]{3,2,1,0:T(8,128)} fusion(f32[5,68,37,128]{3,2,1,0:T(8,128)} %multiply_subtract_fusion.4, f32[5,69,36,128]{3,2,1,0:T(8,128)} %multiply_subtract_fusion, f32[5,68,36,128]{3,2,1,0:T(8,128)} %copy-done.3, f32[5,68,36,127]{3,2,1,0:T(8,128)} %bitcast.223, f32[5,68,36,1]{3,2,1,0:T(8,128)} %slice.750, f32[5,72,40,128]{3,2,1,0:T(8,128)} %pad_maximum_fusion), kind=kLoop, calls=%fused_computation.15 | loop fusion | flops 14100480 | bytes 50135040 | tf_op jit(solution)/shard_map/add | solution.py:106
  773.1 12.5 multiply_add_fusion.3
  785.6 17.4 multiply_add_fusion.5
  818.9 12.2 multiply_subtract_fusion.10
  863.2 12.3 multiply_subtract_fusion.8
  881.2 12.0 multiply_subtract_fusion.6
  893.2 20.3 %fusion.11 = f32[5,64,32,128]{3,2,1,0:T(8,128)} fusion(f32[5,64,32,128]{3,2,1,0:T(8,128)} %reshape.525, f32[5,64,33,128]{3,2,1,0:T(8,128)} %multiply_subtract_fusion.6, f32[5,65,32,128]{3,2,1,0:T(8,128)} %multiply_subtract_fusion.8, f32[5,64,32,128]{3,2,1,0:T(8,128)} %multiply_subtract_fusion.10, f32[5,64,32,127]{3,2,1,0:T(8,128)} %bitcast.230, ...), kind=kLoop, calls=%fused_computation.51 | loop fusion | flops 14417920 | bytes 47185920 | tf_op jit(solution)/shard_map/add | solution.py:108
  944.3 51.8 %all_to_all.38 = f32[8,1,65536]{2,1,0:T(1,128)} all-to-all(f32[8,1,65536]{2,1,0:T(1,128)S(1)} %reshape.554), channel_id=1, replica_groups=mesh['row'=4,'col'=8] {'col'}, dimensions={0} | all-to-all | bytes 4194304 | tf_op jit(solution)/shard_map/all_to_all | solution.py:218
  1029.4 24.6 %all-to-all-done.2 = f32[4,2,64,1024]{3,2,1,0:T(8,128)} async-done(((f32[4,2,64,1024]{3,2,1,0:T(8,128)}), f32[4,2,64,1024]{3,2,1,0:T(8,128)}, u32[]{:S(2)}, u32[]{:S(2)}) %all-to-all-start.2) | async-done | bytes 2097184 | tf_op jit(solution)/shard_map/all_to_all | solution.py:229
  1149.4 77.3 %all_to_all.39 = f32[4,1,393216]{2,1,0:T(1,128)} all-to-all(f32[4,1,393216]{2,1,0:T(1,128)} %reshape.556), channel_id=1, replica_groups=mesh['row'=4,'col'=8] {'row'}, dimensions={0} | all-to-all | bytes 12582912 | tf_op jit(solution)/shard_map/all_to_all | solution.py:275
  1226.7 20.9 %reduce.1 = f32[4,393216]{1,0:T(4,128)} reduce(f32[4,1,393216]{2,1,0:T(1,128)} %all_to_all.39, f32[]{:T(128)} %broadcast.990), dimensions={1}, to_apply=%all_to_all.28.reduce_sub_computation | reduce | bytes 12582916 | tf_op jit(solution)/shard_map/all_to_all | solution.py:275
  1247.6 13.1 reshape.557
  1281.4 11.9 reshape.529
  1314.5 141.7 %all_to_all.40 = f32[8,3,2,32,1024]{4,3,1,2,0:T(8,128)} all-to-all(f32[8,3,2,32,1024]{4,3,1,2,0:T(8,128)S(1)} %copy_bitcast_fusion), channel_id=1, replica_groups=mesh['row'=4,'col'=8] {'col'}, dimensions={0} | all-to-all | bytes 12582912 | tf_op jit(solution)/shard_map/all_to_all | solution.py:284
  1515.4 14.9 concatenate.61
  1539.6 28.4 %maximum_bitcast_fusion = f32[4,2,8,5,16,16,16]{6,2,5,1,4,0,3:T(8,128)} fusion(f32[1,4,16,2,16,8,16]{6,5,4,3,2,1,0:T(8,128)} %concatenate.62, f32[3,4,16,2,16,8,16]{6,5,4,3,2,1,0:T(8,128)} %concatenate.61, f32[1,4,16,2,16,8,16]{6,5,4,3,2,1,0:T(8,128)} %concatenate.60), kind=kLoop, calls=%fused_computation | loop fusion | flops 2621440 | bytes 10485760 | tf_op jit(solution)/shard_map/transpose | solution.py:294
  1568.1 34.3 %copy.77 = f32[4,2,8,5,16,16,16]{6,5,4,3,2,1,0:T(8,128)} copy(f32[4,2,8,5,16,16,16]{6,2,5,1,4,0,3:T(8,128)} %maximum_bitcast_fusion) | data formatting | bytes 10485760 | tf_op jit(solution)/shard_map/transpose | solution.py:294
  1602.4 62.1 %reshape.550 = f32[64,20480,1]{1,0,2:T(8,128)} reshape(f32[4,2,8,5,16,16,16]{6,5,4,3,2,1,0:T(8,128)} %copy.77) | data formatting | bytes 10485760 | tf_op jit(solution)/shard_map/reshape | solution.py:295
  1670.9 231.5 %all_to_all.41 = f32[8,16,20480]{2,1,0:T(8,128)} all-to-all(f32[8,16,20480]{2,1,0:T(8,128)S(1)} %fusion.102), channel_id=1, replica_groups=mesh['row'=4,'col'=8] {'col'}, dimensions={0} | all-to-all | bytes 20971520 | tf_op jit(solution)/shard_map/all_to_all | solution.py:298
  1902.4 11.7 copy.78
  (310 shorter events, 530.9 us)
Async XLA Ops:
  2.6 510.4 %copy-start.28 = (s32[8,16]{1,0:T(8,128)}, s32[8,16]{1,0:T(8,128)S(1)}, u32[]{:S(2)}) copy-start(s32[8,16]{1,0:T(8,128)S(1)} %multiply_add_fusion.6) | copy-start | bytes 1540
  17.2 11.3 copy-start.30
  17.2 11.2 copy-start.32
  40.2 230.5 %all-to-all-start = ((f32[8,16,20480]{2,1,0:T(8,128)}), f32[8,16,20480]{2,1,0:T(8,128)}, u32[]{:S(2)}, u32[]{:S(2)}) async-start(f32[8,16,20480]{2,1,0:T(8,128)} %fusion.99), calls=%async_computation | async-start | bytes 20971520 | tf_op jit(solution)/shard_map/all_to_all | solution.py:196
  494.1 8.2 collective-permute-start
  494.2 11.2 collective-permute-start.1
  508.2 33.5 %collective-permute-start.2 = (f32[5,72,4,128]{3,2,1,0:T(4,128)S(1)}, f32[5,72,4,128]{3,2,1,0:T(4,128)S(1)}, u32[]{:S(2)}, u32[]{:S(2)}) collective-permute-start(f32[5,72,4,128]{3,2,1,0:T(4,128)S(1)} %get-tuple-element.71), channel_id=1, source_target_pairs={{0,1},{1,2},{2,3},{3,4},{4,5},{5,6},{6,7},{7,0},{8,9},{9,10},{10,1... | collective-permute-start | bytes 2211848 | tf_op jit(solution)/shard_map/ppermute | solution.py:26
  509.7 34.2 %collective-permute-start.3 = (f32[5,72,4,128]{3,2,1,0:T(4,128)S(1)}, f32[5,72,4,128]{3,2,1,0:T(4,128)S(1)}, u32[]{:S(2)}, u32[]{:S(2)}) collective-permute-start(f32[5,72,4,128]{3,2,1,0:T(4,128)S(1)} %get-tuple-element.72), channel_id=1, source_target_pairs={{1,0},{2,1},{3,2},{4,3},{5,4},{6,5},{7,6},{0,7},{9,8},{10,9},{11,1... | collective-permute-start | bytes 2211848 | tf_op jit(solution)/shard_map/ppermute | solution.py:29
  573.4 7.8 copy-start
  654.8 12.6 slice-start.10
  660.2 7.2 slice-start.11
  660.2 10.4 slice-start.8
  661.8 8.8 slice-start.9
  739.2 10.4 copy-start.1
  837.4 7.7 slice-start.14
  838.9 6.2 slice-start.15
  845.2 6.5 slice-start.7
  918.9 6.4 copy-start.9
  1023.6 30.4 %all-to-all-start.2 = ((f32[4,2,64,1024]{3,2,1,0:T(8,128)}), f32[4,2,64,1024]{3,2,1,0:T(8,128)}, u32[]{:S(2)}, u32[]{:S(2)}) async-start(f32[4,2,64,1024]{3,2,1,0:T(8,128)} %maximum_bitcast_fusion.3), calls=%async_computation.2 | async-start | bytes 4194304 | tf_op jit(solution)/shard_map/all_to_all | solution.py:229
  1085.0 7.8 copy-start.13
  1085.0 7.8 copy-start.15
  1085.0 7.8 copy-start.17
  1104.5 6.2 copy-start.16
  1104.5 6.2 copy-start.18
  1116.1 12.8 slice-start.18
  1293.4 6.4 copy-start.5
  1498.9 12.9 slice-start.16
  1505.5 6.3 slice-start.17
  1602.4 62.1 %copy-start.29 = (s32[8,16]{1,0:T(8,128)S(1)}, s32[8,16]{1,0:T(8,128)}, u32[]{:S(2)}) copy-start(s32[8,16]{1,0:T(8,128)} %copy-done.28) | copy-start | bytes 1540
  1602.4 62.1 %copy-start.34 = (s32[64]{0:T(128)S(1)}, s32[64]{0:T(128)}, u32[]{:S(2)}) copy-start(s32[64]{0:T(128)} %get-tuple-element.91) | copy-start | bytes 772
  1902.4 11.8 copy-start.31
  1902.4 11.8 copy-start.33
  (29 other events, 110.5 us)
where the time goes:
time: 1930 us
  blocking collectives  515 us (27%)
  local copies, waits for them, and re-layouts  498 us (26%)
  other arithmetic  348 us (18%)
  waiting for transfers between devices  285 us (15%)
  matrix products  261 us (14%)
    all_to_all x1, blocking collectives, on_device(): lax.all_to_all(return_buffer, 'col', split_axis=0, concat_axis=0, tiled=T...  232 us
    all_to_all x1, waiting for transfers between devices, on_device(): lax.all_to_all(send_buffer, 'col', split_axis=0, concat_axis=0, tiled=True)  224 us
    all_to_all x2, blocking collectives, on_device(): lax.all_to_all(packed, 'col', split_axis=0, concat_axis=0, tiled=True)  194 us
    dot_general x1, matrix products, on_device(): jnp.matmul(recv_select, arrived, precision=lax.Precision.HIGHEST)  155 us
    unnamed x134, local copies, waits for them, and re-layouts  96.2 us
    add x6, other arithmetic, face_rates(): centre + 0.5 * minmod_slope(centre - lower_cell, upper_cell - centre)  88.5 us
    all_to_all x1, blocking collectives, on_device(): lax.all_to_all(packed, 'row', split_axis=0, concat_axis=0, tiled=True)  77.3 us
    reshape x1, local copies, waits for them, and re-layouts, on_device(): back_bricks = kicked.reshape(5, lat_x, PE, per_pencil_y, brick_y, lat_z,...  62.1 us
  transfers between devices with their start and end apart: 6, of which 5 were waited for; matrix products, arithmetic and copies ran while one was open for 0% of the time, Pallas kernels for 0%

commit v1 on v0

v1 whole, which is shorter than its diff:
```python
import functools
import math

import jax
import jax.numpy as jnp
import numpy as np
from jax import lax
from jax.experimental import pallas as pl
from jax.experimental.pallas import tpu as pltpu
from jax.sharding import PartitionSpec as P

PE = 16
GX = 256
GY = 256
GZ = 128
LANES = 128
SUB = 8
VMEM_BYTES = 56 * 1024 * 1024


gamma_gas = 1.4
speed_bound = 4.0
time_step = 0.03
four_pi_g = 10.0


def shift_pair(axis):
    count = lax.axis_size(axis)
    forward = [(i, (i + 1) % count) for i in range(count)]
    backward = [(target, source) for source, target in forward]
    return forward, backward


def edges(block, axis, dim, width):
    forward, backward = shift_pair(axis)
    low = lax.ppermute(
        lax.slice_in_dim(block, block.shape[dim] - width, None, axis=dim), axis, forward
    )
    high = lax.ppermute(lax.slice_in_dim(block, 0, width, axis=dim), axis, backward)
    return low, high


def padded(block, sides, width):
    for axis, dim in sides:
        low, high = edges(block, axis, dim, width)
        block = jnp.concatenate([low, block, high], axis=dim)
    return block


def half_flux(state, direction):
    density, momenta, energy = state[0], state[1:4], state[4]
    inverse = 1.0 / density
    velocity = momenta[direction] * inverse
    kinetic = (
        0.5
        * (momenta[0] * momenta[0] + momenta[1] * momenta[1] + momenta[2] * momenta[2])
        * inverse
    )
    pressure = (gamma_gas - 1.0) * (energy - kinetic)
    half_velocity = 0.5 * velocity
    pieces = [0.5 * momenta[direction]]
    for component in range(3):
        term = momenta[component] * half_velocity
        if component == direction:
            term = term + 0.5 * pressure
        pieces.append(term)
    pieces.append((energy + pressure) * half_velocity)
    return pieces


def side_terms(lower_gap, centre, upper_gap, direction):
    left, right = [], []
    for low, mid, high in zip(lower_gap, centre, upper_gap):
        slope = jnp.maximum(jnp.minimum(low, high), 0.0) + jnp.minimum(
            jnp.maximum(low, high), 0.0
        )
        left.append(mid + 0.5 * slope)
        right.append(mid - 0.5 * slope)
    damping = 0.5 * speed_bound
    below = [f + damping * u for f, u in zip(half_flux(left, direction), left)]
    above = [f - damping * u for f, u in zip(half_flux(right, direction), right)]
    return below, above


def step_kernel(ext_ref, out_ref, first_ref, part_ref, last_ref):
    planes = ext_ref.shape[1]
    depth_y = ext_ref.shape[2]
    out_y = out_ref.shape[2]

    def plane(ref, i):
        return [ref[q, i] for q in range(5)]

    def x_terms(ref, i):
        low, mid, high = plane(ref, i - 1), plane(ref, i), plane(ref, i + 1)
        return side_terms(
            [m - l for l, m in zip(low, mid)], mid, [h - m for m, h in zip(mid, high)], 0
        )

    def begin(ref, i):
        before, _ = x_terms(ref, i - 1)
        below, above = x_terms(ref, i)
        for q in range(5):
            last_ref[q] = below[q]
            part_ref[q] = below[q] - above[q] - before[q]

    def change(ref, i):
        below, above = x_terms(ref, i + 1)
        total = []
        for q in range(5):
            total.append(part_ref[q] + above[q])
            part_ref[q] = below[q] - above[q] - last_ref[q]
            last_ref[q] = below[q]
        mid = plane(ref, i)
        for direction, axis, size in ((1, 0, depth_y), (2, 1, LANES)):
            upper_gap = [pltpu.roll(m, size - 1, axis) - m for m in mid]
            lower_gap = [pltpu.roll(g, 1, axis) for g in upper_gap]
            below, above = side_terms(lower_gap, mid, upper_gap, direction)
            total = [
                t + (b - a) + (pltpu.roll(a, size - 1, axis) - pltpu.roll(b, 1, axis))
                for t, b, a in zip(total, below, above)
            ]
        return mid, total

    begin(ext_ref, 2)

    def first_step(i, carry):
        mid, total = change(ext_ref, i)
        for q in range(5):
            first_ref[q, i] = mid[q] - time_step * total[q]
        return carry

    lax.fori_loop(2, planes - 2, first_step, 0)
    begin(first_ref, 4)

    def second_step(i, carry):
        mid, total = change(first_ref, i)
        for q in range(5):
            value = 0.5 * ext_ref[q, i] + 0.5 * (mid[q] - time_step * total[q])
            out_ref[q, i - 4] = pltpu.roll(value, depth_y - 4, 0)[:out_y]
        return carry

    lax.fori_loop(4, planes - 4, second_step, 0)


def advance(extended):
    _, planes, depth_y, depth_z = extended.shape
    out_shape = (5, planes - 8, depth_y - 8, depth_z)
    cells = planes * depth_y * depth_z
    return pl.pallas_call(
        step_kernel,
        out_shape=jax.ShapeDtypeStruct(out_shape, jnp.float32),
        in_specs=[pl.BlockSpec(memory_space=pltpu.VMEM)],
        out_specs=pl.BlockSpec(memory_space=pltpu.VMEM),
        scratch_shapes=[
            pltpu.VMEM((5, planes, depth_y, depth_z), jnp.float32),
            pltpu.VMEM((5, depth_y, depth_z), jnp.float32),
            pltpu.VMEM((5, depth_y, depth_z), jnp.float32),
        ],
        compiler_params=pltpu.CompilerParams(vmem_limit_bytes=VMEM_BYTES),
        cost_estimate=pl.CostEstimate(
            flops=900 * cells, bytes_accessed=40 * cells, transcendentals=0
        ),
        name="gas_step",
    )(extended)


def pack_kernel(block_y, brick_y, start_ref, in_ref, out_ref):
    cols_count, _, repeat_y = out_ref.shape[:3]
    halves = brick_y // SUB
    per_patch = PE // brick_y
    stride = PE * halves
    lat_y = in_ref.shape[0]
    offset = lax.rem(start_ref[0], lat_y)

    def one(i, carry):
        peer = i // repeat_y
        inner = lax.rem(i, repeat_y)
        y_patch = peer * block_y // PE + inner
        slot = lax.rem(y_patch - offset + lat_y, lat_y)
        brick = lax.rem(peer, per_patch)
        for row in range(stride):
            a, half = divmod(row, halves)
            lane = (2 * a + half) * LANES
            if per_patch > 1:
                lane = pl.multiple_of(lane + brick * halves * LANES, LANES)
            out_ref[peer, 0, inner, pl.ds(row, 5, stride=stride), :] = in_ref[
                slot, :, pl.ds(lane, LANES)
            ]
        return carry

    lax.fori_loop(0, cols_count * repeat_y, one, 0)


def pack_slots(fields, own_start, cols_count, block_y, brick_y, lat_y, repeat_y):
    capacity = fields.shape[0]
    groups = capacity // lat_y
    rows = 5 * PE * (brick_y // SUB)
    return pl.pallas_call(
        functools.partial(pack_kernel, block_y, brick_y),
        out_shape=jax.ShapeDtypeStruct(
            (cols_count, groups, repeat_y, rows, LANES), jnp.float32
        ),
        grid_spec=pltpu.PrefetchScalarGridSpec(
            num_scalar_prefetch=1,
            grid=(groups,),
            in_specs=[pl.BlockSpec((lat_y, 5, PE * PE * PE), lambda g, s: (g, 0, 0))],
            out_specs=pl.BlockSpec(
                (cols_count, 1, repeat_y, rows, LANES), lambda g, s: (0, g, 0, 0, 0)
            ),
        ),
        compiler_params=pltpu.CompilerParams(vmem_limit_bytes=VMEM_BYTES),
        name="pack_slots",
    )(own_start.reshape(1), fields)


def unpack_kernel(block_y, brick_y, info_ref, in_ref, out_ref):
    repeat_y = in_ref.shape[2]
    halves = brick_y // SUB
    per_patch = PE // brick_y
    stride = PE * halves
    lat_y = out_ref.shape[0]
    base = pl.program_id(0) * lat_y

    def one(t, carry):
        y_patch = lax.rem(info_ref[0] + t, lat_y)
        live = jnp.full((5, LANES), base + t, jnp.int32) < info_ref[1]
        inner = lax.rem(y_patch, repeat_y)
        for brick in range(per_patch):
            peer = (y_patch * PE + brick * brick_y) // block_y
            for row in range(stride):
                a, half = divmod(row, halves)
                lane = (2 * a + brick * halves + half) * LANES
                value = in_ref[peer, 0, inner, pl.ds(row, 5, stride=stride), :]
                out_ref[t, :, pl.ds(lane, LANES)] = jnp.where(live, value, 0.0)
        return carry

    lax.fori_loop(0, lat_y, one, 0)


def unpack_slots(arrived, own_start, own_count, block_y, brick_y, lat_y):
    cols_count, groups, repeat_y, rows, _ = arrived.shape
    return pl.pallas_call(
        functools.partial(unpack_kernel, block_y, brick_y),
        out_shape=jax.ShapeDtypeStruct((groups * lat_y, 5, PE * PE * PE), jnp.float32),
        grid_spec=pltpu.PrefetchScalarGridSpec(
            num_scalar_prefetch=1,
            grid=(groups,),
            in_specs=[
                pl.BlockSpec(
                    (cols_count, 1, repeat_y, rows, LANES), lambda g, s: (0, g, 0, 0, 0)
                )
            ],
            out_specs=pl.BlockSpec((lat_y, 5, PE * PE * PE), lambda g, s: (g, 0, 0)),
        ),
        compiler_params=pltpu.CompilerParams(vmem_limit_bytes=VMEM_BYTES),
        name="unpack_slots",
    )(jnp.stack([own_start, own_count]), arrived)


def swap_blocks(values):
    lane = lax.broadcasted_iota(jnp.int32, (SUB, LANES), 1)
    count = len(values)
    step = 1
    while step < count:
        shift = step * PE
        low = (lane // shift) % 2 == 0
        swapped = list(values)
        for i in range(count):
            if i & step == 0:
                one, two = values[i], values[i | step]
                swapped[i] = jnp.where(low, one, pltpu.roll(two, shift, 1))
                swapped[i | step] = jnp.where(low, pltpu.roll(one, LANES - shift, 1), two)
        values = swapped
        step *= 2
    return values


def gather_kernel(index_ref, *refs):
    lat_z = GZ // PE
    in_refs, out_ref, rows_ref = refs[:lat_z], refs[lat_z], refs[lat_z + 1]
    brick_y = out_ref.shape[3]
    groups = in_refs[0].shape[1] // SUB

    def regroup(m, carry):
        at = pl.multiple_of(m * SUB, SUB)
        values = swap_blocks([ref[0, pl.ds(at, SUB), :] for ref in in_refs])
        for b in range(SUB):
            rows_ref[pl.ds(m * (SUB * SUB) + b, SUB, stride=SUB), :] = values[b]
        return carry

    lax.fori_loop(0, groups, regroup, 0)
    for q in range(5):

        def place(a, carry):
            at = pl.multiple_of((q * PE + a) * brick_y, SUB)
            out_ref[q, a, 0] = rows_ref[pl.ds(at, brick_y), :]
            return carry

        lax.fori_loop(0, PE, place, 0)


def gather_bricks(arrived, source_index, lat_x, per_pencil_y, brick_y):
    lat_z = GZ // PE
    rows = arrived.shape[1]

    def picked(zl):
        return lambda i, w, index: (index[(i * per_pencil_y + w) * lat_z + zl], 0, 0)

    out = pl.pallas_call(
        gather_kernel,
        out_shape=jax.ShapeDtypeStruct(
            (5, lat_x * PE, per_pencil_y, brick_y, LANES), jnp.float32
        ),
        grid_spec=pltpu.PrefetchScalarGridSpec(
            num_scalar_prefetch=1,
            grid=(lat_x, per_pencil_y),
            in_specs=[pl.BlockSpec((1, rows, LANES), picked(zl)) for zl in range(lat_z)],
            out_specs=pl.BlockSpec(
                (5, PE, 1, brick_y, LANES), lambda i, w, index: (0, i, w, 0, 0)
            ),
            scratch_shapes=[pltpu.VMEM((rows * SUB, LANES), jnp.float32)],
        ),
        compiler_params=pltpu.CompilerParams(vmem_limit_bytes=VMEM_BYTES),
        name="gather_bricks",
    )(source_index, *([arrived] * lat_z))
    return out.reshape(5, lat_x * PE, per_pencil_y * brick_y, GZ)


def kick_kernel(index_ref, state_ref, gradient_ref, out_ref, rows_ref, brick_ref, sems):
    lat_z = GZ // PE
    brick_y = state_ref.shape[3]
    groups = brick_ref.shape[1] // SUB
    at_grid = (pl.program_id(0) * pl.num_programs(1) + pl.program_id(1)) * lat_z

    def kick(a, carry):
        density = state_ref[0, a, 0]
        momenta = [state_ref[1 + d, a, 0] for d in range(3)]
        slopes = [gradient_ref[d, a, 0] for d in range(3)]
        work = momenta[0] * slopes[0] + momenta[1] * slopes[1] + momenta[2] * slopes[2]
        pieces = [density]
        for d in range(3):
            pieces.append(momenta[d] - time_step * density * slopes[d])
        pieces.append(state_ref[4, a, 0] - time_step * work)
        for q in range(5):
            at = pl.multiple_of((q * PE + a) * brick_y, SUB)
            rows_ref[pl.ds(at, brick_y), :] = pieces[q]
        return carry

    lax.fori_loop(0, PE, kick, 0)

    def regroup(m, carry):
        at = pl.multiple_of(m * SUB, SUB)
        values = swap_blocks(
            [rows_ref[pl.ds(m * (SUB * SUB) + b, SUB, stride=SUB), :] for b in range(SUB)]
        )
        for zl in range(lat_z):
            brick_ref[zl, pl.ds(at, SUB), :] = values[zl]
        return carry

    lax.fori_loop(0, groups, regroup, 0)
    copies = [
        pltpu.make_async_copy(
            brick_ref.at[zl], out_ref.at[index_ref[at_grid + zl]], sems.at[zl]
        )
        for zl in range(lat_z)
    ]
    for copy in copies:
        copy.start()
    for copy in copies:
        copy.wait()


def kick_bricks(stepped, gradient, source_index, buffer_rows, lat_x, per_pencil_y, brick_y):
    lat_z = GZ // PE
    rows = 5 * PE * (brick_y // SUB)
    shape = (lat_x * PE, per_pencil_y, brick_y, GZ)

    def block(count):
        return pl.BlockSpec((count, PE, 1, brick_y, GZ), lambda i, w, index: (0, i, w, 0, 0))

    return pl.pallas_call(
        kick_kernel,
        out_shape=jax.ShapeDtypeStruct((buffer_rows, rows, LANES), jnp.float32),
        grid_spec=pltpu.PrefetchScalarGridSpec(
            num_scalar_prefetch=1,
            grid=(lat_x, per_pencil_y),
            in_specs=[block(5), block(3)],
            out_specs=pl.BlockSpec(memory_space=pl.ANY),
            scratch_shapes=[
                pltpu.VMEM((rows * SUB, LANES), jnp.float32),
                pltpu.VMEM((lat_z, rows, LANES), jnp.float32),
                pltpu.SemaphoreType.DMA((lat_z,)),
            ],
        ),
        compiler_params=pltpu.CompilerParams(vmem_limit_bytes=VMEM_BYTES),
        name="kick_bricks",
    )(source_index, stepped.reshape((5,) + shape), gradient.reshape((3,) + shape))


def lap_eigen(wave, length):
    return 2.0 * jnp.cos(2.0 * math.pi / length * wave) - 2.0


def hartley(length):
    indices = np.arange(length)
    angles = 2.0 * np.pi / length * (indices[:, None] * indices[None, :] % length)
    return jnp.asarray((np.cos(angles) + np.sin(angles)).astype(np.float32))


def matmul(a, b):
    return jnp.matmul(a, b, precision=lax.Precision.HIGHEST)


def exchange(packed, axis):
    return lax.all_to_all(packed, axis, split_axis=0, concat_axis=0, tiled=True)


def solve_potential(density, my_row, my_column, rows_count, cols_count):
    block_x, block_y, _ = density.shape
    rows_y = GY // rows_count
    cols_z = GZ // cols_count
    table_x, table_y, table_z = hartley(GX), hartley(GY), hartley(GZ)
    along = matmul(density.reshape(block_x * block_y, GZ), table_z)
    packed = along.reshape(block_x, block_y, cols_count, cols_z).transpose(2, 1, 3, 0)
    mid = exchange(packed.reshape(GY, cols_z * block_x), "col")
    spectrum = exchange(matmul(table_y, mid), "row")
    spectrum = (
        spectrum.reshape(rows_count, rows_y, cols_z, block_x)
        .transpose(1, 2, 0, 3)
        .reshape(rows_y * cols_z, GX)
    )
    spectrum = matmul(spectrum, table_x)
    index_x = jnp.arange(GX, dtype=jnp.int32)
    index_y = my_row * rows_y + jnp.arange(rows_y, dtype=jnp.int32)
    index_z = my_column * cols_z + jnp.arange(cols_z, dtype=jnp.int32)
    eigen = (
        lap_eigen(index_x.astype(jnp.float32), GX)[None, None, :]
        + lap_eigen(index_y.astype(jnp.float32), GY)[:, None, None]
        + lap_eigen(index_z.astype(jnp.float32), GZ)[None, :, None]
    )
    zero_mode = (
        (index_x == 0)[None, None, :]
        & (index_y == 0)[:, None, None]
        & (index_z == 0)[None, :, None]
    )
    scale = 1.0 / (GX * GY * GZ)
    green = jnp.where(
        zero_mode, 0.0, four_pi_g * scale / jnp.where(zero_mode, -1.0, eigen)
    ).reshape(rows_y * cols_z, GX)
    back = matmul(spectrum * green, table_x)
    packed = back.reshape(rows_y, cols_z, rows_count, block_x).transpose(2, 0, 1, 3)
    mid = exchange(packed.reshape(GY, cols_z * block_x), "row")
    returned = exchange(matmul(table_y, mid), "col")
    returned = (
        returned.reshape(cols_count, block_y, cols_z, block_x)
        .transpose(3, 1, 0, 2)
        .reshape(block_x * block_y, GZ)
    )
    return matmul(returned, table_z).reshape(block_x, block_y, GZ)


def potential_gradient(potential):
    low_x, high_x = edges(potential, "row", 0, 1)
    low_y, high_y = edges(potential, "col", 1, 1)
    wide_x = jnp.concatenate([low_x, potential, high_x], axis=0)
    wide_y = jnp.concatenate([low_y, potential, high_y], axis=1)
    return jnp.stack(
        [
            0.5 * (wide_x[2:] - wide_x[:-2]),
            0.5 * (wide_y[:, 2:] - wide_y[:, :-2]),
            0.5 * (jnp.roll(potential, -1, 2) - jnp.roll(potential, 1, 2)),
        ]
    )


def on_device(fields, counts):
    rows_count = lax.axis_size("row")
    cols_count = lax.axis_size("col")
    my_row = lax.axis_index("row")
    my_column = lax.axis_index("col")
    capacity = fields.shape[0]
    block_x = GX // rows_count
    block_y = GY // cols_count
    lat_x = block_x // PE
    lat_y = GY // PE
    lat_z = GZ // PE
    brick_y = min(PE, block_y)
    per_pencil_y = block_y // brick_y
    repeat_y = max(1, block_y // PE)
    per_peer = capacity // lat_y * repeat_y
    rows = 5 * PE * (brick_y // SUB)
    buffer_rows = cols_count * per_peer
    row_counts = lax.all_gather(counts, "col", axis=1, tiled=True).reshape(cols_count)
    starts = jnp.cumsum(row_counts) - row_counts
    column_ids = jnp.arange(cols_count, dtype=jnp.int32)
    own_start = jnp.sum(jnp.where(column_ids == my_column, starts, 0)).astype(jnp.int32)
    own_count = counts[0, 0]
    grid_xl = jnp.arange(lat_x, dtype=jnp.int32)[:, None, None]
    grid_w = jnp.arange(per_pencil_y, dtype=jnp.int32)[None, :, None]
    grid_zl = jnp.arange(lat_z, dtype=jnp.int32)[None, None, :]
    pencil_y = (my_column * block_y + grid_w * brick_y) // PE
    curve_pos = (grid_xl * lat_z + grid_zl) * lat_y + pencil_y
    curve_pos = curve_pos.reshape(-1)
    y_flat = jnp.broadcast_to(pencil_y, (lat_x, per_pencil_y, lat_z)).reshape(-1)
    owner = jnp.sum((starts[None, :] <= curve_pos[:, None]).astype(jnp.int32), axis=1) - 1
    owner_start = jnp.sum(
        jnp.where(column_ids[None, :] == owner[:, None], starts[None, :], 0), axis=1
    )
    source_index = (
        owner * per_peer + (curve_pos - owner_start) // lat_y * repeat_y + y_flat % repeat_y
    ).astype(jnp.int32)
    send_buffer = pack_slots(
        fields, own_start, cols_count, block_y, brick_y, lat_y, repeat_y
    )
    arrived = exchange(send_buffer.reshape(buffer_rows, rows, LANES), "col")
    pencil = gather_bricks(arrived, source_index, lat_x, per_pencil_y, brick_y)
    extended = padded(pencil, (("row", 1), ("col", 2)), 4)
    stepped = advance(extended)
    potential = solve_potential(stepped[0], my_row, my_column, rows_count, cols_count)
    return_buffer = kick_bricks(
        stepped,
        potential_gradient(potential),
        source_index,
        buffer_rows,
        lat_x,
        per_pencil_y,
        brick_y,
    )
    came_back = exchange(return_buffer, "col").reshape(send_buffer.shape)
    return unpack_slots(came_back, own_start, own_count, block_y, brick_y, lat_y)


def solution(mesh):
    return jax.shard_map(
        on_device,
        mesh=mesh,
        in_specs=(P(("row", "col"), None, None), P("row", "col")),
        out_specs=P(("row", "col"), None, None),
        check_vma=False,
    )
```

time: 1930 us -> 903 us (0.47)
  blocking collectives: 515 us -> 59 us
  local copies, waits for them, and re-layouts: 498 us -> 58.8 us
  other arithmetic: 348 us -> 14.2 us
  waiting for transfers between devices: 285 us -> 532 us
  matrix products: 261 us -> 19.6 us
  Pallas kernels: 0 us -> 183 us
    all_to_all x4 -> x2, blocking collectives: 502 us -> 45.9 us  [exchange(): return lax.all_to_all(packed, axis, split_axis=0, concat_axis=0, tiled=True)]
    dot_general x24 -> x6, matrix products: 261 us -> 19.6 us  [matmul(): return jnp.matmul(a, b, precision=lax.Precision.HIGHEST)]
    all_to_all x2 -> x4, waiting for transfers between devices: 249 us -> 488 us  [exchange(): return lax.all_to_all(packed, axis, split_axis=0, concat_axis=0, tiled=True)]
    pallas_call x0 -> x5, Pallas kernels: none -> 183 us  [the longest x1 63.2 us: advance(): pl.pallas_call(step_kernel, out_shape=jax.ShapeDtypeStruct(out_shape, jnp...]
    add x10 -> x1, other arithmetic: 132 us -> 0.07 us  [solve_potential(): lap_eigen(index_x.astype(jnp.float32), GX)[None, None, :]]
    reshape x7 -> x5, local copies, waits for them, and re-layouts: 131 us -> 9.06 us  [the longest x1 3.63 us: solve_potential(): returned = returned.reshape(cols_count, block_y, cols_z, block_x).transpo...]
    slice x17 -> x5, local copies, waits for them, and re-layouts: 95 us -> 2.06 us  [the longest x1 1.28 us: edges(): lax.slice_in_dim(block, block.shape[dim] - width, None, axis=dim)]
    transpose x5 -> x2, local copies, waits for them, and re-layouts: 92.6 us -> 6.97 us  [the longest x1 4.3 us: solve_potential(): along.reshape(block_x, block_y, cols_count, cols_z).transpose(2, 1, 3, 0)]
  transfers between devices with their start and end apart: 6 -> 12, of which waited for: 5 -> 11; matrix products, arithmetic and copies ran while one was open for 0% -> 1% of each run, Pallas kernels for 0% -> 0%
where the time goes in v1:
time: 903 us; the launch traced here: 895 us
  waiting for transfers between devices  532 us (59%)
  Pallas kernels  183 us (20%)
  blocking collectives  59 us (7%)
  local copies, waits for them, and re-layouts  58.8 us (7%)
  starting transfers between devices  27.7 us (3%)
  matrix products  19.6 us (2%)
  other arithmetic  14.2 us (2%)
    all_to_all x4, waiting for transfers between devices, exchange(): return lax.all_to_all(packed, axis, split_axis=0, concat_axis=0, tiled=True)  488 us
    pallas_call x1, Pallas kernels, advance(): pl.pallas_call(step_kernel, out_shape=jax.ShapeDtypeStruct(out_shape, jnp...  63.2 us
    all_to_all x2, blocking collectives, exchange(): return lax.all_to_all(packed, axis, split_axis=0, concat_axis=0, tiled=True)  45.9 us
    pallas_call x1, Pallas kernels, kick_bricks(): pl.pallas_call(kick_kernel, out_shape=jax.ShapeDtypeStruct((buffer_rows,...  45.3 us
    pallas_call x1, Pallas kernels, gather_bricks(): pl.pallas_call(gather_kernel, out_shape=jax.ShapeDtypeStruct((5, lat_x *...  42.9 us
    ppermute x4, waiting for transfers between devices, edges(): lax.ppermute(lax.slice_in_dim(block, block.shape[dim] - width, None, axis...  40.3 us
    dot_general x6, matrix products, matmul(): return jnp.matmul(a, b, precision=lax.Precision.HIGHEST)  19.6 us
    unnamed x14, local copies, waits for them, and re-layouts  18.1 us
  transfers between devices with their start and end apart: 12, of which 11 were waited for; matrix products, arithmetic and copies ran while one was open for 1% of the time, Pallas kernels for 0%

profile of v1, /device:TPU:0, one launch (start us, length us, event | category | flops | bytes accessed | tf_op | source)
XLA Modules:
  0.0 895.4 jit_solution(2678967433122035500)
XLA Ops:
  2.6 13.1 %all-reduce = s32[8]{0:T(128)S(1)} all-reduce(s32[8]{0:T(128)S(1)} %bitcast_dynamic-update-slice_fusion), channel_id=1, replica_groups=mesh['row'=4,'col'=8] {'col'}, use_global_device_ids=true, to_apply=%add | all-reduce | flops 8 | bytes 64 | tf_op jit(solution)/shard_map/reshape | solution.py:493
  15.8 16.2 %copy.19.in_ref = f32[128,5,4096]{2,1,0:T(8,128)} copy(f32[128,5,4096]{2,0,1:T(8,128)} %param.5) | data formatting | bytes 20971520 | tf_op args[0]
  32.6 15.2 %pack_slots.1 = f32[8,8,2,160,128]{4,3,2,1,0:T(8,128)} custom-call(s32[1]{0:T(128)} %bitcast.4.start_ref, f32[128,5,4096]{2,1,0:T(8,128)} %copy.19.in_ref), custom_call_target="tpu_custom_call" | custom-call | tf_op jit(solution)/shard_map/pack_slots/pallas_call | solution.py:198
  47.9 5.2 all-to-all-start
  54.1 224.3 %all-to-all-done.refs_0_.refs_1_.refs_2_.refs_3_.refs_4_.refs_5_.refs_6_.refs_7_ = f32[128,160,128]{2,1,0:T(8,128)} async-done(((f32[128,160,128]{2,1,0:T(8,128)}), f32[128,160,128]{2,1,0:T(8,128)}, u32[]{:S(2)}, u32[]{:S(2)}) %all-to-all-start) | async-done | bytes 10485792 | tf_op jit(solution)/shard_map/all_to_all | solution.py:415
  278.4 42.9 %gather_bricks.1 = f32[5,64,2,16,128]{4,3,2,1,0:T(8,128)} custom-call(s32[64]{0:T(128)} %fusion.8.index_ref, f32[128,160,128]{2,1,0:T(8,128)} %all-to-all-done.refs_0_.refs_1_.refs_2_.refs_3_.refs_4_.refs_5_.refs_6_.refs_7_, f32[128,160,128]{2,1,0:T(8,128)} %all-to-all-done.refs_0_.refs_1_.refs_2_.refs_3_.refs_4_.refs_5_.refs_6_.refs_7_, ...), custom_call_target="tpu_custom_call" | custom-call | tf_op jit(solution)/shard_map/gather_bricks/pallas_call | solution.py:309
  324.4 6.4 collective-permute-done
  331.7 2.0 pad_maximum_fusion.8
  335.3 3.8 collective-permute-start.3
  339.1 28.7 %collective-permute-done.2 = f32[5,72,4,128]{3,2,1,0:T(4,128)S(1)} collective-permute-done((f32[5,72,4,128]{3,2,1,0:T(4,128)S(1)}, f32[5,72,4,128]{3,2,1,0:T(4,128)S(1)}, u32[]{:S(2)}, u32[]{:S(2)}) %collective-permute-start.2) | collective-permute-done | bytes 737312 | tf_op jit(solution)/shard_map/ppermute | solution.py:36
  367.8 2.7 collective-permute-done.3
  370.5 4.7 pad_maximum_fusion.ext_ref
  375.2 63.2 %gas_step.1 = f32[5,64,32,128]{3,2,1,0:T(8,128)} custom-call(f32[5,72,40,128]{3,2,1,0:T(8,128)} %pad_maximum_fusion.ext_ref), custom_call_target="tpu_custom_call" | custom-call | flops 331776000 | bytes 14745600 | tf_op jit(solution)/shard_map/gas_step/pallas_call | solution.py:149
  438.4 12.8 %convolution_bitcast_fusion = f32[8,32,16,64]{1,2,0,3:T(8,128)} fusion(f32[8,16,128,1]{2,1,0,3:T(8,128)S(1)} %copy-done.4, f32[5,64,32,128]{3,2,1,0:T(8,128)} %gas_step.1), kind=kOutput, calls=%fused_computation.2 | convolution fusion | flops 402653184 | bytes 2162688 | tf_op jit(solution)/shard_map/dot_general | solution.py:411
  451.2 4.3 copy.20
  457.1 3.6 all-to-all-start.1
  460.8 25.7 %all-to-all-done.1 = f32[8,32,1024]{2,1,0:T(8,128)S(1)} async-done(((f32[8,32,1024]{2,1,0:T(8,128)}), f32[8,32,1024]{2,1,0:T(8,128)S(1)}, u32[]{:S(2)}, u32[]{:S(2)}) %all-to-all-start.1) | async-done | bytes 1048608 | tf_op jit(solution)/shard_map/all_to_all | solution.py:415
  488.5 3.7 all-to-all-start.2
  493.9 12.7 %all-to-all-done.2 = f32[4,64,1024]{2,1,0:T(8,128)S(1)} async-done(((f32[4,64,1024]{2,1,0:T(8,128)}), f32[4,64,1024]{2,1,0:T(8,128)S(1)}, u32[]{:S(2)}, u32[]{:S(2)}) %all-to-all-start.2) | async-done | bytes 1048608 | tf_op jit(solution)/shard_map/all_to_all | solution.py:415
  507.2 2.7 copy.21
  509.9 2.5 reshape.334
  518.8 16.9 %all_to_all.52 = f32[4,64,1024]{2,1,0:T(8,128)S(1)} all-to-all(f32[4,64,1024]{2,1,0:T(8,128)S(1)} %all_to_all.40), channel_id=1, replica_groups=mesh['row'=4,'col'=8] {'row'}, dimensions={0} | all-to-all | bytes 2097152 | tf_op jit(solution)/shard_map/all_to_all | solution.py:415
  536.7 29.1 %all_to_all.53 = f32[8,32,1024]{2,1,0:T(8,128)S(1)} all-to-all(f32[8,32,1024]{2,1,0:T(8,128)S(1)} %bitcast.104), channel_id=1, replica_groups=mesh['row'=4,'col'=8] {'col'}, dimensions={0} | all-to-all | bytes 2097152 | tf_op jit(solution)/shard_map/all_to_all | solution.py:415
  565.7 2.7 copy.23
  568.5 3.6 reshape.337
  574.7 2.3 collective-permute-start.6
  580.2 3.4 collective-permute-done.7
  586.0 45.3 %kick_bricks.1 = f32[128,160,128]{2,1,0:T(8,128)} custom-call(s32[64]{0:T(128)} %fusion.8.index_ref, f32[5,64,2,16,128]{4,3,2,1,0:T(8,128)} %bitcast.92, f32[3,64,2,16,128]{4,3,2,1,0:T(8,128)} %pad_maximum_fusion.1.gradient_ref), custom_call_target="tpu_custom_call" | custom-call | tf_op jit(solution)/shard_map/kick_bricks/pallas_call | solution.py:381
  631.3 5.4 all-to-all-start.5
  638.0 225.1 %all-to-all-done.5 = f32[128,160,128]{2,1,0:T(8,128)} async-done(((f32[128,160,128]{2,1,0:T(8,128)}), f32[128,160,128]{2,1,0:T(8,128)}, u32[]{:S(2)}, u32[]{:S(2)}) %all-to-all-start.5) | async-done | bytes 10485792 | tf_op jit(solution)/shard_map/all_to_all | solution.py:415
  863.1 16.0 %unpack_slots.1 = f32[128,5,4096]{2,1,0:T(8,128)} custom-call(s32[2]{0:T(128)} %pad_add_fusion.info_ref, f32[8,8,2,160,128]{4,3,2,1,0:T(8,128)} %bitcast.35.in_ref), custom_call_target="tpu_custom_call" | custom-call | tf_op jit(solution)/shard_map/unpack_slots/pallas_call | solution.py:242
  879.2 15.9 %copy.24 = f32[128,5,4096]{2,0,1:T(8,128)} copy(f32[128,5,4096]{2,1,0:T(8,128)} %unpack_slots.1) | data formatting | bytes 20971520 | tf_op jit(solution)/shard_map/unpack_slots/pallas_call | solution.py:242
  (70 shorter events, 31.9 us)
Async XLA Ops:
  47.9 230.6 %all-to-all-start = ((f32[128,160,128]{2,1,0:T(8,128)}), f32[128,160,128]{2,1,0:T(8,128)}, u32[]{:S(2)}, u32[]{:S(2)}) async-start(f32[128,160,128]{2,1,0:T(8,128)} %bitcast.87), calls=%async_computation | async-start | bytes 20971520 | tf_op jit(solution)/shard_map/all_to_all | solution.py:415
  321.3 49.2 %copy-start = (f32[5,64,2,16,128]{4,3,2,1,0:T(8,128)S(1)}, f32[5,64,2,16,128]{4,3,2,1,0:T(8,128)}, u32[]{:S(2)}) copy-start(f32[5,64,2,16,128]{4,3,2,1,0:T(8,128)} %gather_bricks.1) | copy-start | bytes 15728644
  322.6 8.2 collective-permute-start
  322.7 9.0 %collective-permute-start.1 = (f32[5,4,32,128]{3,2,1,0:T(8,128)S(1)}, f32[5,4,32,128]{3,2,1,0:T(8,128)S(1)}, u32[]{:S(2)}, u32[]{:S(2)}) collective-permute-start(f32[5,4,32,128]{3,2,1,0:T(8,128)S(1)} %get-tuple-element.8), channel_id=1, source_target_pairs={{8,0},{16,8},{24,16},{0,24},{9,1},{17,9},{25,17},{1,25},{10,2},{18... | collective-permute-start | bytes 983048 | tf_op jit(solution)/shard_map/ppermute | solution.py:39
  333.8 34.0 %collective-permute-start.2 = (f32[5,72,4,128]{3,2,1,0:T(4,128)S(1)}, f32[5,72,4,128]{3,2,1,0:T(4,128)S(1)}, u32[]{:S(2)}, u32[]{:S(2)}) collective-permute-start(f32[5,72,4,128]{3,2,1,0:T(4,128)S(1)} %get-tuple-element.5), channel_id=1, source_target_pairs={{0,1},{1,2},{2,3},{3,4},{4,5},{5,6},{6,7},{7,0},{8,9},{9,10},{10,1... | collective-permute-start | bytes 2211848 | tf_op jit(solution)/shard_map/ppermute | solution.py:36
  335.3 35.2 %collective-permute-start.3 = (f32[5,72,4,128]{3,2,1,0:T(4,128)S(1)}, f32[5,72,4,128]{3,2,1,0:T(4,128)S(1)}, u32[]{:S(2)}, u32[]{:S(2)}) collective-permute-start(f32[5,72,4,128]{3,2,1,0:T(4,128)S(1)} %get-tuple-element.6), channel_id=1, source_target_pairs={{1,0},{2,1},{3,2},{4,3},{5,4},{6,5},{7,6},{0,7},{9,8},{10,9},{11,1... | collective-permute-start | bytes 2211848 | tf_op jit(solution)/shard_map/ppermute | solution.py:39
  375.2 63.2 %copy-start.4 = (f32[8,16,128,1]{2,1,0,3:T(8,128)S(1)}, f32[8,16,128,1]{2,1,0,3:T(8,128)}, u32[]{:S(2)}) copy-start(f32[8,16,128,1]{2,1,0,3:T(8,128)} %constant.102) | copy-start | bytes 196612
  451.2 35.3 %copy-start.2 = (f32[256,256]{1,0:T(8,128)S(1)}, f32[256,256]{1,0:T(8,128)}, u32[]{:S(2)}) copy-start(f32[256,256]{1,0:T(8,128)} %constant.91.clone) | copy-start | bytes 786436
  457.1 29.4 %all-to-all-start.1 = ((f32[8,32,1024]{2,1,0:T(8,128)}), f32[8,32,1024]{2,1,0:T(8,128)S(1)}, u32[]{:S(2)}, u32[]{:S(2)}) async-start(f32[8,32,1024]{2,1,0:T(8,128)} %all_to_all.35), calls=%async_computation.1 | async-start | bytes 2097152 | tf_op jit(solution)/shard_map/all_to_all | solution.py:415
  488.5 18.1 %all-to-all-start.2 = ((f32[4,64,1024]{2,1,0:T(8,128)}), f32[4,64,1024]{2,1,0:T(8,128)S(1)}, u32[]{:S(2)}, u32[]{:S(2)}) async-start(f32[4,64,1024]{2,1,0:T(8,128)} %bitcast.17), calls=%async_computation.2 | async-start | bytes 2097152 | tf_op jit(solution)/shard_map/all_to_all | solution.py:415
  507.2 5.2 copy-start.1
  565.7 6.3 copy-start.3
  574.7 5.5 collective-permute-start.6
  577.1 6.6 collective-permute-start.7
  577.1 1.4 collective-permute-start.4
  577.1 3.2 collective-permute-start.5
  631.3 231.8 %all-to-all-start.5 = ((f32[128,160,128]{2,1,0:T(8,128)}), f32[128,160,128]{2,1,0:T(8,128)}, u32[]{:S(2)}, u32[]{:S(2)}) async-start(f32[128,160,128]{2,1,0:T(8,128)} %kick_bricks.1), calls=%async_computation.5 | async-start | bytes 20971520 | tf_op jit(solution)/shard_map/all_to_all | solution.py:415

commit v2 on v1

--- a/solution.py
+++ b/solution.py
@@ -15,6 +15,7 @@
 GZ = 128
 LANES = 128
 SUB = 8
+TOGETHER = 5
 VMEM_BYTES = 56 * 1024 * 1024
 
 
@@ -24,9 +25,22 @@
 four_pi_g = 10.0
 
 
+def ring_order(axis):
+    count = lax.axis_size(axis)
+    if axis == "col" and count == 8:
+        return [0, 2, 4, 6, 7, 5, 3, 1]
+    return list(range(count))
+
+
+def block_of(axis):
+    order = ring_order(axis)
+    return [order.index(i) for i in range(len(order))]
+
+
 def shift_pair(axis):
-    count = lax.axis_size(axis)
-    forward = [(i, (i + 1) % count) for i in range(count)]
+    order = ring_order(axis)
+    count = len(order)
+    forward = [(order[i], order[(i + 1) % count]) for i in range(count)]
     backward = [(target, source) for source, target in forward]
     return forward, backward
 
@@ -164,84 +178,109 @@
     )(extended)
 
 
-def pack_kernel(block_y, brick_y, start_ref, in_ref, out_ref):
-    cols_count, _, repeat_y = out_ref.shape[:3]
-    halves = brick_y // SUB
-    per_patch = PE // brick_y
-    stride = PE * halves
-    lat_y = in_ref.shape[0]
+def pack_kernel(start_ref, in_ref, out_ref, rows_ref):
+    cols_count, _, repeat_y, rows, _ = out_ref.shape
+    lat_y = in_ref.shape[1]
+    bricks = cols_count * repeat_y
+    per_patch = bricks // lat_y
+    halves = 2 // per_patch
     offset = lax.rem(start_ref[0], lat_y)
 
-    def one(i, carry):
-        peer = i // repeat_y
-        inner = lax.rem(i, repeat_y)
-        y_patch = peer * block_y // PE + inner
-        slot = lax.rem(y_patch - offset + lat_y, lat_y)
-        brick = lax.rem(peer, per_patch)
-        for row in range(stride):
-            a, half = divmod(row, halves)
-            lane = (2 * a + half) * LANES
-            if per_patch > 1:
-                lane = pl.multiple_of(lane + brick * halves * LANES, LANES)
-            out_ref[peer, 0, inner, pl.ds(row, 5, stride=stride), :] = in_ref[
-                slot, :, pl.ds(lane, LANES)
-            ]
-        return carry
-
-    lax.fori_loop(0, cols_count * repeat_y, one, 0)
-
-
-def pack_slots(fields, own_start, cols_count, block_y, brick_y, lat_y, repeat_y):
+    for q in range(5):
+
+        def chunk(a, carry):
+            for brick in range(per_patch):
+                for half in range(halves):
+                    lane = pl.multiple_of((2 * a + brick * halves + half) * LANES, LANES)
+                    value = pltpu.roll(in_ref[q, :, pl.ds(lane, LANES)], offset, 0)
+                    row = brick * rows + (q * PE + a) * halves + half
+                    for part in range(lat_y // SUB):
+                        rows_ref[
+                            pl.ds(
+                                part * SUB * per_patch * rows + row,
+                                SUB,
+                                stride=per_patch * rows,
+                            ),
+                            :,
+                        ] = value[part * SUB : (part + 1) * SUB]
+            return carry
+
+        lax.fori_loop(0, PE, chunk, 0, unroll=4)
+
+    for i, block in enumerate(block_of("col")):
+        for inner in range(repeat_y):
+            out_ref[i, 0, inner] = rows_ref[pl.ds((block * repeat_y + inner) * rows, rows), :]
+
+
+def pack_slots(fields, own_start, cols_count, brick_y, lat_y, repeat_y):
     capacity = fields.shape[0]
     groups = capacity // lat_y
     rows = 5 * PE * (brick_y // SUB)
     return pl.pallas_call(
-        functools.partial(pack_kernel, block_y, brick_y),
+        pack_kernel,
         out_shape=jax.ShapeDtypeStruct(
             (cols_count, groups, repeat_y, rows, LANES), jnp.float32
         ),
         grid_spec=pltpu.PrefetchScalarGridSpec(
             num_scalar_prefetch=1,
             grid=(groups,),
-            in_specs=[pl.BlockSpec((lat_y, 5, PE * PE * PE), lambda g, s: (g, 0, 0))],
+            in_specs=[pl.BlockSpec((5, lat_y, PE * PE * PE), lambda g, s: (0, g, 0))],
             out_specs=pl.BlockSpec(
                 (cols_count, 1, repeat_y, rows, LANES), lambda g, s: (0, g, 0, 0, 0)
             ),
+            scratch_shapes=[pltpu.VMEM((cols_count * repeat_y * rows, LANES), jnp.float32)],
         ),
         compiler_params=pltpu.CompilerParams(vmem_limit_bytes=VMEM_BYTES),
         name="pack_slots",
-    )(own_start.reshape(1), fields)
-
-
-def unpack_kernel(block_y, brick_y, info_ref, in_ref, out_ref):
-    repeat_y = in_ref.shape[2]
-    halves = brick_y // SUB
-    per_patch = PE // brick_y
-    stride = PE * halves
-    lat_y = out_ref.shape[0]
-    base = pl.program_id(0) * lat_y
-
-    def one(t, carry):
-        y_patch = lax.rem(info_ref[0] + t, lat_y)
-        live = jnp.full((5, LANES), base + t, jnp.int32) < info_ref[1]
-        inner = lax.rem(y_patch, repeat_y)
-        for brick in range(per_patch):
-            peer = (y_patch * PE + brick * brick_y) // block_y
-            for row in range(stride):
-                a, half = divmod(row, halves)
-                lane = (2 * a + brick * halves + half) * LANES
-                value = in_ref[peer, 0, inner, pl.ds(row, 5, stride=stride), :]
-                out_ref[t, :, pl.ds(lane, LANES)] = jnp.where(live, value, 0.0)
-        return carry
-
-    lax.fori_loop(0, lat_y, one, 0)
-
-
-def unpack_slots(arrived, own_start, own_count, block_y, brick_y, lat_y):
+    )(own_start.reshape(1), fields.transpose(1, 0, 2))
+
+
+def unpack_kernel(info_ref, in_ref, out_ref, rows_ref):
+    cols_count, _, repeat_y, rows, _ = in_ref.shape
+    lat_y = out_ref.shape[1]
+    bricks = cols_count * repeat_y
+    per_patch = bricks // lat_y
+    halves = 2 // per_patch
+    offset = lax.rem(lat_y - lax.rem(info_ref[0], lat_y), lat_y)
+    for i, block in enumerate(block_of("col")):
+        for inner in range(repeat_y):
+            rows_ref[pl.ds((block * repeat_y + inner) * rows, rows), :] = in_ref[i, 0, inner]
+    slot = pl.program_id(0) * lat_y + lax.broadcasted_iota(jnp.int32, (lat_y, LANES), 0)
+    live = slot < info_ref[1]
+
+    for q in range(5):
+
+        def chunk(a, carry):
+            for brick in range(per_patch):
+                for half in range(halves):
+                    lane = pl.multiple_of((2 * a + brick * halves + half) * LANES, LANES)
+                    row = brick * rows + (q * PE + a) * halves + half
+                    value = jnp.concatenate(
+                        [
+                            rows_ref[
+                                pl.ds(
+                                    part * SUB * per_patch * rows + row,
+                                    SUB,
+                                    stride=per_patch * rows,
+                                ),
+                                :,
+                            ]
+                            for part in range(lat_y // SUB)
+                        ],
+                        axis=0,
+                    )
+                    value = pltpu.roll(value, offset, 0)
+                    out_ref[q, :, pl.ds(lane, LANES)] = jnp.where(live, value, 0.0)
+            return carry
+
+        lax.fori_loop(0, PE, chunk, 0, unroll=4)
+
+
+def unpack_slots(arrived, own_start, own_count, lat_y):
     cols_count, groups, repeat_y, rows, _ = arrived.shape
-    return pl.pallas_call(
-        functools.partial(unpack_kernel, block_y, brick_y),
-        out_shape=jax.ShapeDtypeStruct((groups * lat_y, 5, PE * PE * PE), jnp.float32),
+    out = pl.pallas_call(
+        unpack_kernel,
+        out_shape=jax.ShapeDtypeStruct((5, groups * lat_y, PE * PE * PE), jnp.float32),
         grid_spec=pltpu.PrefetchScalarGridSpec(
             num_scalar_prefetch=1,
             grid=(groups,),
@@ -250,29 +289,33 @@
                     (cols_count, 1, repeat_y, rows, LANES), lambda g, s: (0, g, 0, 0, 0)
                 )
             ],
-            out_specs=pl.BlockSpec((lat_y, 5, PE * PE * PE), lambda g, s: (g, 0, 0)),
+            out_specs=pl.BlockSpec((5, lat_y, PE * PE * PE), lambda g, s: (0, g, 0)),
+            scratch_shapes=[pltpu.VMEM((cols_count * repeat_y * rows, LANES), jnp.float32)],
         ),
         compiler_params=pltpu.CompilerParams(vmem_limit_bytes=VMEM_BYTES),
         name="unpack_slots",
     )(jnp.stack([own_start, own_count]), arrived)
-
-
-def swap_blocks(values):
+    return out.transpose(1, 0, 2)
+
+
+def swap_many(many):
     lane = lax.broadcasted_iota(jnp.int32, (SUB, LANES), 1)
-    count = len(values)
     step = 1
-    while step < count:
+    while step < GZ // PE:
         shift = step * PE
         low = (lane // shift) % 2 == 0
-        swapped = list(values)
-        for i in range(count):
-            if i & step == 0:
-                one, two = values[i], values[i | step]
-                swapped[i] = jnp.where(low, one, pltpu.roll(two, shift, 1))
-                swapped[i | step] = jnp.where(low, pltpu.roll(one, LANES - shift, 1), two)
-        values = swapped
+        result = []
+        for values in many:
+            swapped = list(values)
+            for i, one in enumerate(values):
+                if i & step == 0:
+                    two = values[i | step]
+                    swapped[i] = jnp.where(low, one, pltpu.roll(two, shift, 1))
+                    swapped[i | step] = jnp.where(low, pltpu.roll(one, LANES - shift, 1), two)
+            result.append(swapped)
+        many = result
         step *= 2
-    return values
+    return many
 
 
 def gather_kernel(index_ref, *refs):
@@ -281,22 +324,21 @@
     brick_y = out_ref.shape[3]
     groups = in_refs[0].shape[1] // SUB
 
-    def regroup(m, carry):
-        at = pl.multiple_of(m * SUB, SUB)
-        values = swap_blocks([ref[0, pl.ds(at, SUB), :] for ref in in_refs])
-        for b in range(SUB):
-            rows_ref[pl.ds(m * (SUB * SUB) + b, SUB, stride=SUB), :] = values[b]
+    def regroup(n, carry):
+        firsts = [n * TOGETHER + m for m in range(TOGETHER)]
+        values = [
+            [ref[0, pl.ds(pl.multiple_of(m * SUB, SUB), SUB), :] for ref in in_refs]
+            for m in firsts
+        ]
+        for m, swapped in zip(firsts, swap_many(values)):
+            for b in range(SUB):
+                rows_ref[pl.ds(m * (SUB * SUB) + b, SUB, stride=SUB), :] = swapped[b]
         return carry
 
-    lax.fori_loop(0, groups, regroup, 0)
+    lax.fori_loop(0, groups // TOGETHER, regroup, 0)
     for q in range(5):
-
-        def place(a, carry):
-            at = pl.multiple_of((q * PE + a) * brick_y, SUB)
-            out_ref[q, a, 0] = rows_ref[pl.ds(at, brick_y), :]
-            return carry
-
-        lax.fori_loop(0, PE, place, 0)
+        for a in range(PE):
+            out_ref[q, a, 0] = rows_ref[pl.ds((q * PE + a) * brick_y, brick_y), :]
 
 
 def gather_bricks(arrived, source_index, lat_x, per_pencil_y, brick_y):
@@ -346,18 +388,20 @@
             rows_ref[pl.ds(at, brick_y), :] = pieces[q]
         return carry
 
-    lax.fori_loop(0, PE, kick, 0)
-
-    def regroup(m, carry):
-        at = pl.multiple_of(m * SUB, SUB)
-        values = swap_blocks(
+    lax.fori_loop(0, PE, kick, 0, unroll=4)
+
+    def regroup(n, carry):
+        firsts = [n * TOGETHER + m for m in range(TOGETHER)]
+        values = [
             [rows_ref[pl.ds(m * (SUB * SUB) + b, SUB, stride=SUB), :] for b in range(SUB)]
-        )
-        for zl in range(lat_z):
-            brick_ref[zl, pl.ds(at, SUB), :] = values[zl]
+            for m in firsts
+        ]
+        for m, swapped in zip(firsts, swap_many(values)):
+            for zl in range(lat_z):
+                brick_ref[zl, pl.ds(pl.multiple_of(m * SUB, SUB), SUB), :] = swapped[zl]
         return carry
 
-    lax.fori_loop(0, groups, regroup, 0)
+    lax.fori_loop(0, groups // TOGETHER, regroup, 0)
     copies = [
         pltpu.make_async_copy(
             brick_ref.at[zl], out_ref.at[index_ref[at_grid + zl]], sems.at[zl]
@@ -420,10 +464,13 @@
     rows_y = GY // rows_count
     cols_z = GZ // cols_count
     table_x, table_y, table_z = hartley(GX), hartley(GY), hartley(GZ)
+    table_y = jnp.concatenate(
+        [table_y[block * block_y : (block + 1) * block_y] for block in block_of("col")]
+    )
     along = matmul(density.reshape(block_x * block_y, GZ), table_z)
     packed = along.reshape(block_x, block_y, cols_count, cols_z).transpose(2, 1, 3, 0)
     mid = exchange(packed.reshape(GY, cols_z * block_x), "col")
-    spectrum = exchange(matmul(table_y, mid), "row")
+    spectrum = exchange(matmul(table_y.T, mid), "row")
     spectrum = (
         spectrum.reshape(rows_count, rows_y, cols_z, block_x)
         .transpose(1, 2, 0, 3)
@@ -495,10 +542,12 @@
     column_ids = jnp.arange(cols_count, dtype=jnp.int32)
     own_start = jnp.sum(jnp.where(column_ids == my_column, starts, 0)).astype(jnp.int32)
     own_count = counts[0, 0]
+    block_ids = jnp.array(block_of("col"), jnp.int32)
+    my_block = jnp.sum(jnp.where(column_ids == my_column, block_ids, 0)).astype(jnp.int32)
     grid_xl = jnp.arange(lat_x, dtype=jnp.int32)[:, None, None]
     grid_w = jnp.arange(per_pencil_y, dtype=jnp.int32)[None, :, None]
     grid_zl = jnp.arange(lat_z, dtype=jnp.int32)[None, None, :]
-    pencil_y = (my_column * block_y + grid_w * brick_y) // PE
+    pencil_y = (my_block * block_y + grid_w * brick_y) // PE
     curve_pos = (grid_xl * lat_z + grid_zl) * lat_y + pencil_y
     curve_pos = curve_pos.reshape(-1)
     y_flat = jnp.broadcast_to(pencil_y, (lat_x, per_pencil_y, lat_z)).reshape(-1)
@@ -509,9 +558,7 @@
     source_index = (
         owner * per_peer + (curve_pos - owner_start) // lat_y * repeat_y + y_flat % repeat_y
     ).astype(jnp.int32)
-    send_buffer = pack_slots(
-        fields, own_start, cols_count, block_y, brick_y, lat_y, repeat_y
-    )
+    send_buffer = pack_slots(fields, own_start, cols_count, brick_y, lat_y, repeat_y)
     arrived = exchange(send_buffer.reshape(buffer_rows, rows, LANES), "col")
     pencil = gather_bricks(arrived, source_index, lat_x, per_pencil_y, brick_y)
     extended = padded(pencil, (("row", 1), ("col", 2)), 4)
@@ -527,7 +574,7 @@
         brick_y,
     )
     came_back = exchange(return_buffer, "col").reshape(send_buffer.shape)
-    return unpack_slots(came_back, own_start, own_count, block_y, brick_y, lat_y)
+    return unpack_slots(came_back, own_start, own_count, lat_y)
 
 
 def solution(mesh):

time: 903 us -> 784 us (0.87)
  Pallas kernels: 183 us -> 122 us
  local copies, waits for them, and re-layouts: 58.8 us -> 26.7 us
  waiting for transfers between devices: 532 us -> 516 us
    ppermute x4, waiting for transfers between devices: 40.3 us -> 5.35 us  [edges(): lax.ppermute(lax.slice_in_dim(block, block.shape[dim] - width, None, axis...]
    pallas_call x1, Pallas kernels: 42.9 us -> 12.4 us  [gather_bricks(): pl.pallas_call(gather_kernel, out_shape=jax.ShapeDtypeStruct((5, lat_x *...]
    pallas_call x1, Pallas kernels: 45.3 us -> 17.3 us  [kick_bricks(): pl.pallas_call(kick_kernel, out_shape=jax.ShapeDtypeStruct((buffer_rows,...]
    ppermute x4, waiting for transfers between devices: 3.95 us -> 24.1 us  [edges(): lax.ppermute(lax.slice_in_dim(block, 0, width, axis=dim), axis, backward)]
    unnamed x14 -> x17, local copies, waits for them, and re-layouts: 18.1 us -> 1.95 us
    pallas_call x1 -> x0, local copies, waits for them, and re-layouts: 15.9 us -> none  [unpack_slots(): pl.pallas_call(functools.partial(unpack_kernel, block_y, brick_y), out_sh...]
  transfers between devices with their start and end apart: 12 -> 12, of which waited for: 11 -> 10; matrix products, arithmetic and copies ran while one was open for 1% -> 1% of each run, Pallas kernels for 0% -> 0%
where the time goes in v2:
time: 784 us; the launch traced here: 783 us
  waiting for transfers between devices  516 us (66%)
  Pallas kernels  122 us (16%)
  blocking collectives  58.6 us (7%)
  local copies, waits for them, and re-layouts  26.7 us (3%)
  starting transfers between devices  24 us (3%)
  matrix products  19.6 us (3%)
  other arithmetic  14.9 us (2%)
    all_to_all x4, waiting for transfers between devices, exchange(): return lax.all_to_all(packed, axis, split_axis=0, concat_axis=0, tiled=True)  486 us
    pallas_call x1, Pallas kernels, advance(): pl.pallas_call(step_kernel, out_shape=jax.ShapeDtypeStruct(out_shape, jnp...  63.2 us
    all_to_all x2, blocking collectives, exchange(): return lax.all_to_all(packed, axis, split_axis=0, concat_axis=0, tiled=True)  45.5 us
    ppermute x4, waiting for transfers between devices, edges(): lax.ppermute(lax.slice_in_dim(block, 0, width, axis=dim), axis, backward)  24.1 us
    dot_general x6, matrix products, matmul(): return jnp.matmul(a, b, precision=lax.Precision.HIGHEST)  19.6 us
    all_to_all x4, starting transfers between devices, exchange(): return lax.all_to_all(packed, axis, split_axis=0, concat_axis=0, tiled=True)  17.6 us
    pallas_call x1, Pallas kernels, kick_bricks(): pl.pallas_call(kick_kernel, out_shape=jax.ShapeDtypeStruct((buffer_rows,...  17.3 us
  transfers between devices with their start and end apart: 12, of which 10 were waited for; matrix products, arithmetic and copies ran while one was open for 1% of the time, Pallas kernels for 0%

profile of v2, /device:TPU:0, one launch (start us, length us, event | category | flops | bytes accessed | tf_op | source)
XLA Modules:
  0.0 782.7 jit_solution(7303895839045798254)
XLA Ops:
  2.6 13.1 %all-reduce = s32[8]{0:T(128)S(1)} all-reduce(s32[8]{0:T(128)S(1)} %bitcast_dynamic-update-slice_fusion), channel_id=1, replica_groups=mesh['row'=4,'col'=8] {'col'}, use_global_device_ids=true, to_apply=%add | all-reduce | flops 8 | bytes 64 | tf_op jit(solution)/shard_map/reshape | solution.py:540
  17.2 14.9 %pack_slots.1 = f32[8,8,2,160,128]{4,3,2,1,0:T(8,128)} custom-call(s32[1]{0:T(128)} %bitcast.4.start_ref, f32[5,128,4096]{2,1,0:T(8,128)} %bitcast.100), custom_call_target="tpu_custom_call" | custom-call | tf_op jit(solution)/shard_map/pack_slots/pallas_call | solution.py:219
  32.0 5.2 all-to-all-start
  38.9 223.7 %all-to-all-done.refs_0_.refs_1_.refs_2_.refs_3_.refs_4_.refs_5_.refs_6_.refs_7_ = f32[128,160,128]{2,1,0:T(8,128)} async-done(((f32[128,160,128]{2,1,0:T(8,128)}), f32[128,160,128]{2,1,0:T(8,128)}, u32[]{:S(2)}, u32[]{:S(2)}) %all-to-all-start) | async-done | bytes 10485792 | tf_op jit(solution)/shard_map/all_to_all | solution.py:459
  262.6 12.4 %gather_bricks.1 = f32[5,64,2,16,128]{4,3,2,1,0:T(8,128)} custom-call(s32[64]{0:T(128)} %fusion.9.index_ref, f32[128,160,128]{2,1,0:T(8,128)} %all-to-all-done.refs_0_.refs_1_.refs_2_.refs_3_.refs_4_.refs_5_.refs_6_.refs_7_, f32[128,160,128]{2,1,0:T(8,128)} %all-to-all-done.refs_0_.refs_1_.refs_2_.refs_3_.refs_4_.refs_5_.refs_6_.refs_7_, ...), custom_call_target="tpu_custom_call" | custom-call | tf_op jit(solution)/shard_map/gather_bricks/pallas_call | solution.py:351
  276.8 6.6 collective-permute-done.1
  283.4 3.0 collective-permute-done
  286.4 2.0 pad_maximum_fusion.8
  290.5 16.5 %collective-permute-done.3 = f32[5,72,4,128]{3,2,1,0:T(4,128)S(1)} collective-permute-done((f32[5,72,4,128]{3,2,1,0:T(4,128)S(1)}, f32[5,72,4,128]{3,2,1,0:T(4,128)S(1)}, u32[]{:S(2)}, u32[]{:S(2)}) %collective-permute-start.3) | collective-permute-done | bytes 737312 | tf_op jit(solution)/shard_map/ppermute | solution.py:53
  308.1 4.7 pad_maximum_fusion.ext_ref
  312.8 63.2 %gas_step.1 = f32[5,64,32,128]{3,2,1,0:T(8,128)} custom-call(f32[5,72,40,128]{3,2,1,0:T(8,128)} %pad_maximum_fusion.ext_ref), custom_call_target="tpu_custom_call" | custom-call | flops 331776000 | bytes 14745600 | tf_op jit(solution)/shard_map/gas_step/pallas_call | solution.py:163
  376.0 12.8 %convolution_bitcast_fusion = f32[8,32,16,64]{1,2,0,3:T(8,128)} fusion(f32[8,16,128,1]{2,1,0,3:T(8,128)S(1)} %copy-done.6, f32[5,64,32,128]{3,2,1,0:T(8,128)} %gas_step.1), kind=kOutput, calls=%fused_computation.2 | convolution fusion | flops 402653184 | bytes 2162688 | tf_op jit(solution)/shard_map/dot_general | solution.py:455
  388.8 4.3 copy.11
  394.7 3.6 all-to-all-start.1
  398.5 24.9 %all-to-all-done.1 = f32[8,32,1024]{2,1,0:T(8,128)S(1)} async-done(((f32[8,32,1024]{2,1,0:T(8,128)}), f32[8,32,1024]{2,1,0:T(8,128)S(1)}, u32[]{:S(2)}, u32[]{:S(2)}) %all-to-all-start.1) | async-done | bytes 1048608 | tf_op jit(solution)/shard_map/all_to_all | solution.py:459
  423.4 2.0 fusion.19
  425.4 3.7 all-to-all-start.2
  430.8 12.6 %all-to-all-done.2 = f32[4,64,1024]{2,1,0:T(8,128)S(1)} async-done(((f32[4,64,1024]{2,1,0:T(8,128)}), f32[4,64,1024]{2,1,0:T(8,128)S(1)}, u32[]{:S(2)}, u32[]{:S(2)}) %all-to-all-start.2) | async-done | bytes 1048608 | tf_op jit(solution)/shard_map/all_to_all | solution.py:459
  444.0 2.7 copy.20
  446.6 2.5 reshape.336
  453.6 2.0 all_to_all.35
  455.6 16.9 %all_to_all.46 = f32[4,64,1024]{2,1,0:T(8,128)S(1)} all-to-all(f32[4,64,1024]{2,1,0:T(8,128)S(1)} %all_to_all.35), channel_id=1, replica_groups=mesh['row'=4,'col'=8] {'row'}, dimensions={0} | all-to-all | bytes 2097152 | tf_op jit(solution)/shard_map/all_to_all | solution.py:459
  473.5 28.6 %all_to_all.47 = f32[8,32,1024]{2,1,0:T(8,128)S(1)} all-to-all(f32[8,32,1024]{2,1,0:T(8,128)S(1)} %fusion.21), channel_id=1, replica_groups=mesh['row'=4,'col'=8] {'col'}, dimensions={0} | all-to-all | bytes 2097152 | tf_op jit(solution)/shard_map/all_to_all | solution.py:459
  502.1 2.7 copy.16
  504.8 3.6 reshape.339
  508.5 1.8 fusion.22
  511.2 1.7 collective-permute-start.4
  518.3 2.0 pad_maximum_fusion.1.gradient_ref
  520.2 17.3 %kick_bricks.1 = f32[128,160,128]{2,1,0:T(8,128)} custom-call(s32[64]{0:T(128)} %fusion.9.index_ref, f32[5,64,2,16,128]{4,3,2,1,0:T(8,128)} %bitcast.98, f32[3,64,2,16,128]{4,3,2,1,0:T(8,128)} %pad_maximum_fusion.1.gradient_ref), custom_call_target="tpu_custom_call" | custom-call | tf_op jit(solution)/shard_map/kick_bricks/pallas_call | solution.py:425
  537.5 5.2 all-to-all-start.5
  543.9 224.9 %all-to-all-done.5 = f32[128,160,128]{2,1,0:T(8,128)} async-done(((f32[128,160,128]{2,1,0:T(8,128)}), f32[128,160,128]{2,1,0:T(8,128)}, u32[]{:S(2)}, u32[]{:S(2)}) %all-to-all-start.5) | async-done | bytes 10485792 | tf_op jit(solution)/shard_map/all_to_all | solution.py:459
  768.8 13.9 %unpack_slots.1 = f32[5,128,4096]{2,1,0:T(8,128)} custom-call(s32[2]{0:T(128)} %pad_add_fusion.info_ref, f32[8,8,2,160,128]{4,3,2,1,0:T(8,128)} %bitcast.36.in_ref), custom_call_target="tpu_custom_call" | custom-call | tf_op jit(solution)/shard_map/unpack_slots/pallas_call | solution.py:281
  (72 shorter events, 26.3 us)
Async XLA Ops:
  32.0 230.6 %all-to-all-start = ((f32[128,160,128]{2,1,0:T(8,128)}), f32[128,160,128]{2,1,0:T(8,128)}, u32[]{:S(2)}, u32[]{:S(2)}) async-start(f32[128,160,128]{2,1,0:T(8,128)} %bitcast.93), calls=%async_computation | async-start | bytes 20971520 | tf_op jit(solution)/shard_map/all_to_all | solution.py:459
  275.0 33.1 %copy-start = (f32[5,64,2,16,128]{4,3,2,1,0:T(8,128)S(1)}, f32[5,64,2,16,128]{4,3,2,1,0:T(8,128)}, u32[]{:S(2)}) copy-start(f32[5,64,2,16,128]{4,3,2,1,0:T(8,128)} %gather_bricks.1) | copy-start | bytes 15728644
  276.3 7.2 collective-permute-start.1
  276.3 10.1 %collective-permute-start = (f32[5,4,32,128]{3,2,1,0:T(8,128)S(1)}, f32[5,4,32,128]{3,2,1,0:T(8,128)S(1)}, u32[]{:S(2)}, u32[]{:S(2)}) collective-permute-start(f32[5,4,32,128]{3,2,1,0:T(8,128)S(1)} %get-tuple-element.7), channel_id=1, source_target_pairs={{0,8},{8,16},{16,24},{24,0},{1,9},{9,17},{17,25},{25,1},{2,10},{10... | collective-permute-start | bytes 983048 | tf_op jit(solution)/shard_map/ppermute | solution.py:50
  288.4 18.6 %collective-permute-start.3 = (f32[5,72,4,128]{3,2,1,0:T(4,128)S(1)}, f32[5,72,4,128]{3,2,1,0:T(4,128)S(1)}, u32[]{:S(2)}, u32[]{:S(2)}) collective-permute-start(f32[5,72,4,128]{3,2,1,0:T(4,128)S(1)} %get-tuple-element.6), channel_id=1, source_target_pairs={{2,0},{4,2},{6,4},{7,6},{5,7},{3,5},{1,3},{0,1},{10,8},{12,10},{14... | collective-permute-start | bytes 2211848 | tf_op jit(solution)/shard_map/ppermute | solution.py:53
  290.0 18.1 %collective-permute-start.2 = (f32[5,72,4,128]{3,2,1,0:T(4,128)S(1)}, f32[5,72,4,128]{3,2,1,0:T(4,128)S(1)}, u32[]{:S(2)}, u32[]{:S(2)}) collective-permute-start(f32[5,72,4,128]{3,2,1,0:T(4,128)S(1)} %get-tuple-element.5), channel_id=1, source_target_pairs={{0,2},{2,4},{4,6},{6,7},{7,5},{5,3},{3,1},{1,0},{8,10},{10,12},{12... | collective-permute-start | bytes 2211848 | tf_op jit(solution)/shard_map/ppermute | solution.py:50
  312.8 63.2 %copy-start.6 = (f32[8,16,128,1]{2,1,0,3:T(8,128)S(1)}, f32[8,16,128,1]{2,1,0,3:T(8,128)}, u32[]{:S(2)}) copy-start(f32[8,16,128,1]{2,1,0,3:T(8,128)} %constant.116) | copy-start | bytes 196612
  388.8 34.6 %copy-start.4 = (f32[4,64,256]{2,1,0:T(8,128)S(1)}, f32[4,64,256]{2,1,0:T(8,128)}, u32[]{:S(2)}) copy-start(f32[4,64,256]{2,1,0:T(8,128)} %constant.107) | copy-start | bytes 786436
  394.7 28.8 %all-to-all-start.1 = ((f32[8,32,1024]{2,1,0:T(8,128)}), f32[8,32,1024]{2,1,0:T(8,128)S(1)}, u32[]{:S(2)}, u32[]{:S(2)}) async-start(f32[8,32,1024]{2,1,0:T(8,128)} %all_to_all.31), calls=%async_computation.1 | async-start | bytes 2097152 | tf_op jit(solution)/shard_map/all_to_all | solution.py:459
  425.4 18.0 %all-to-all-start.2 = ((f32[4,64,1024]{2,1,0:T(8,128)}), f32[4,64,1024]{2,1,0:T(8,128)S(1)}, u32[]{:S(2)}, u32[]{:S(2)}) async-start(f32[4,64,1024]{2,1,0:T(8,128)} %fusion.19), calls=%async_computation.2 | async-start | bytes 2097152 | tf_op jit(solution)/shard_map/all_to_all | solution.py:459
  430.8 18.3 %copy-start.2 = (f32[256,256]{1,0:T(8,128)S(1)}, f32[256,256]{1,0:T(8,128)}, u32[]{:S(2)}) copy-start(f32[256,256]{1,0:T(8,128)} %constant.94.clone) | copy-start | bytes 786436
  444.0 5.2 copy-start.1
  452.0 20.4 %copy-start.3 = (f32[8,32,256]{2,1,0:T(8,128)S(1)}, f32[8,32,256]{2,1,0:T(8,128)}, u32[]{:S(2)}) copy-start(f32[8,32,256]{2,1,0:T(8,128)} %constant.105) | copy-start | bytes 786436
  502.1 6.3 copy-start.5
  511.1 4.4 collective-permute-start.5
  511.2 4.4 collective-permute-start.4
  512.9 3.9 collective-permute-start.7
  514.0 3.9 collective-permute-start.6
  537.5 231.3 %all-to-all-start.5 = ((f32[128,160,128]{2,1,0:T(8,128)}), f32[128,160,128]{2,1,0:T(8,128)}, u32[]{:S(2)}, u32[]{:S(2)}) async-start(f32[128,160,128]{2,1,0:T(8,128)} %kick_bricks.1), calls=%async_computation.5 | async-start | bytes 20971520 | tf_op jit(solution)/shard_map/all_to_all | solution.py:459

commit v3 on v2

--- a/solution.py
+++ b/solution.py
@@ -467,7 +467,9 @@
     table_y = jnp.concatenate(
         [table_y[block * block_y : (block + 1) * block_y] for block in block_of("col")]
     )
-    along = matmul(density.reshape(block_x * block_y, GZ), table_z)
+    along = lax.optimization_barrier(
+        matmul(density.reshape(block_x * block_y, GZ), table_z)
+    )
     packed = along.reshape(block_x, block_y, cols_count, cols_z).transpose(2, 1, 3, 0)
     mid = exchange(packed.reshape(GY, cols_z * block_x), "col")
     spectrum = exchange(matmul(table_y.T, mid), "row")
@@ -518,6 +520,20 @@
             0.5 * (jnp.roll(potential, -1, 2) - jnp.roll(potential, 1, 2)),
         ]
     )
+
+
+def all_counts(counts, my_column):
+    cols_count = lax.axis_size("col")
+    if cols_count > 8:
+        return lax.all_gather(counts, "col", axis=1, tiled=True).reshape(cols_count)
+    column_ids = jnp.arange(cols_count, dtype=jnp.int32)
+    result = jnp.where(column_ids == my_column, counts[0, 0], 0)
+    for shift in range(1, cols_count):
+        pairs = [(i, (i + shift) % cols_count) for i in range(cols_count)]
+        arrived = lax.ppermute(counts, "col", pairs)
+        sender = (my_column + cols_count - shift) % cols_count
+        result = result + jnp.where(column_ids == sender, arrived[0, 0], 0)
+    return result
 
 
 def on_device(fields, counts):
@@ -537,7 +553,7 @@
     per_peer = capacity // lat_y * repeat_y
     rows = 5 * PE * (brick_y // SUB)
     buffer_rows = cols_count * per_peer
-    row_counts = lax.all_gather(counts, "col", axis=1, tiled=True).reshape(cols_count)
+    row_counts = all_counts(counts, my_column)
     starts = jnp.cumsum(row_counts) - row_counts
     column_ids = jnp.arange(cols_count, dtype=jnp.int32)
     own_start = jnp.sum(jnp.where(column_ids == my_column, starts, 0)).astype(jnp.int32)

time: 784 us -> 787 us (level)
  blocking collectives: 58.6 us -> 45.5 us
  starting transfers between devices: 24 us -> 36.4 us
  matrix products: 19.6 us -> 7.79 us
  other arithmetic: 14.9 us -> 23.9 us
    reshape x1 -> x0, blocking collectives: 13.1 us -> none  [on_device(): lax.all_gather(counts, 'col', axis=1, tiled=True).reshape(cols_count)]
    ppermute x0 -> x7, starting transfers between devices: none -> 12.4 us  [all_counts(): arrived = lax.ppermute(counts, 'col', pairs)]
    dot_general x6, matrix products: 19.6 us -> 7.79 us  [matmul(): return jnp.matmul(a, b, precision=lax.Precision.HIGHEST)]
  transfers between devices with their start and end apart: 12 -> 19, of which waited for: 10 -> 13; matrix products, arithmetic and copies ran while one was open for 1% -> 1% of each run, Pallas kernels for 0% -> 0%
where the time goes in v3:
time: 787 us; the launch traced here: 785 us
  waiting for transfers between devices  521 us (66%)
  Pallas kernels  122 us (16%)
  blocking collectives  45.5 us (6%)
  starting transfers between devices  36.4 us (5%)
  local copies, waits for them, and re-layouts  26.9 us (3%)
  other arithmetic  23.9 us (3%)
    all_to_all x4, waiting for transfers between devices, exchange(): return lax.all_to_all(packed, axis, split_axis=0, concat_axis=0, tiled=True)  486 us
    pallas_call x1, Pallas kernels, advance(): pl.pallas_call(step_kernel, out_shape=jax.ShapeDtypeStruct(out_shape, jnp...  63.2 us
    all_to_all x2, blocking collectives, exchange(): return lax.all_to_all(packed, axis, split_axis=0, concat_axis=0, tiled=True)  45.5 us
    ppermute x4, waiting for transfers between devices, edges(): lax.ppermute(lax.slice_in_dim(block, 0, width, axis=dim), axis, backward)  24.1 us
    all_to_all x4, starting transfers between devices, exchange(): return lax.all_to_all(packed, axis, split_axis=0, concat_axis=0, tiled=True)  17.6 us
    pallas_call x1, Pallas kernels, kick_bricks(): pl.pallas_call(kick_kernel, out_shape=jax.ShapeDtypeStruct((buffer_rows,...  17.3 us
  transfers between devices with their start and end apart: 19, of which 13 were waited for; matrix products, arithmetic and copies ran while one was open for 1% of the time, Pallas kernels for 0%

profile of v3, /device:TPU:0, one launch (start us, length us, event | category | flops | bytes accessed | tf_op | source)
XLA Modules:
  0.0 784.9 jit_solution(6832607875365925460)
XLA Ops:
  0.0 6.0 collective-permute-start.6
  6.4 3.0 collective-permute-start.3
  18.4 4.5 fusion.15
  23.1 5.8 select_reduce_fusion.2
  28.9 14.8 %pack_slots.1 = f32[8,8,2,160,128]{4,3,2,1,0:T(8,128)} custom-call(s32[1]{0:T(128)} %bitcast.9.start_ref, f32[5,128,4096]{2,1,0:T(8,128)} %bitcast.95), custom_call_target="tpu_custom_call" | custom-call | tf_op jit(solution)/shard_map/pack_slots/pallas_call | solution.py:219
  43.7 5.2 all-to-all-start
  50.6 223.9 %all-to-all-done.refs_0_.refs_1_.refs_2_.refs_3_.refs_4_.refs_5_.refs_6_.refs_7_ = f32[128,160,128]{2,1,0:T(8,128)} async-done(((f32[128,160,128]{2,1,0:T(8,128)}), f32[128,160,128]{2,1,0:T(8,128)}, u32[]{:S(2)}, u32[]{:S(2)}) %all-to-all-start) | async-done | bytes 10485792 | tf_op jit(solution)/shard_map/all_to_all | solution.py:459
  274.5 12.4 %gather_bricks.1 = f32[5,64,2,16,128]{4,3,2,1,0:T(8,128)} custom-call(s32[64]{0:T(128)} %fusion.8.index_ref, f32[128,160,128]{2,1,0:T(8,128)} %all-to-all-done.refs_0_.refs_1_.refs_2_.refs_3_.refs_4_.refs_5_.refs_6_.refs_7_, f32[128,160,128]{2,1,0:T(8,128)} %all-to-all-done.refs_0_.refs_1_.refs_2_.refs_3_.refs_4_.refs_5_.refs_6_.refs_7_, ...), custom_call_target="tpu_custom_call" | custom-call | tf_op jit(solution)/shard_map/gather_bricks/pallas_call | solution.py:351
  288.7 6.6 collective-permute-done.8
  295.3 3.0 collective-permute-done.7
  298.3 2.0 pad_maximum_fusion.8
  302.4 16.5 %collective-permute-done.10 = f32[5,72,4,128]{3,2,1,0:T(4,128)S(1)} collective-permute-done((f32[5,72,4,128]{3,2,1,0:T(4,128)S(1)}, f32[5,72,4,128]{3,2,1,0:T(4,128)S(1)}, u32[]{:S(2)}, u32[]{:S(2)}) %collective-permute-start.10) | collective-permute-done | bytes 737312 | tf_op jit(solution)/shard_map/ppermute | solution.py:53
  320.0 4.7 pad_maximum_fusion.ext_ref
  324.7 63.2 %gas_step.1 = f32[5,64,32,128]{3,2,1,0:T(8,128)} custom-call(f32[5,72,40,128]{3,2,1,0:T(8,128)} %pad_maximum_fusion.ext_ref), custom_call_target="tpu_custom_call" | custom-call | flops 331776000 | bytes 14745600 | tf_op jit(solution)/shard_map/gas_step/pallas_call | solution.py:163
  390.6 2.7 reshape.465
  393.3 3.6 copy.17
  396.9 3.6 all-to-all-start.1
  400.7 24.9 %all-to-all-done.1 = f32[8,32,1024]{2,1,0:T(8,128)S(1)} async-done(((f32[8,32,1024]{2,1,0:T(8,128)}), f32[8,32,1024]{2,1,0:T(8,128)S(1)}, u32[]{:S(2)}, u32[]{:S(2)}) %all-to-all-start.1) | async-done | bytes 1048608 | tf_op jit(solution)/shard_map/all_to_all | solution.py:459
  425.7 2.0 fusion.33
  427.7 3.7 all-to-all-start.2
  433.0 12.6 %all-to-all-done.2 = f32[4,64,1024]{2,1,0:T(8,128)S(1)} async-done(((f32[4,64,1024]{2,1,0:T(8,128)}), f32[4,64,1024]{2,1,0:T(8,128)S(1)}, u32[]{:S(2)}, u32[]{:S(2)}) %all-to-all-start.2) | async-done | bytes 1048608 | tf_op jit(solution)/shard_map/all_to_all | solution.py:459
  446.2 2.7 copy.22
  448.9 2.5 reshape.467
  455.8 2.0 all_to_all.35
  457.8 16.9 %all_to_all.46 = f32[4,64,1024]{2,1,0:T(8,128)S(1)} all-to-all(f32[4,64,1024]{2,1,0:T(8,128)S(1)} %all_to_all.35), channel_id=1, replica_groups=mesh['row'=4,'col'=8] {'row'}, dimensions={0} | all-to-all | bytes 2097152 | tf_op jit(solution)/shard_map/all_to_all | solution.py:459
  475.7 28.6 %all_to_all.47 = f32[8,32,1024]{2,1,0:T(8,128)S(1)} all-to-all(f32[8,32,1024]{2,1,0:T(8,128)S(1)} %fusion.35), channel_id=1, replica_groups=mesh['row'=4,'col'=8] {'col'}, dimensions={0} | all-to-all | bytes 2097152 | tf_op jit(solution)/shard_map/all_to_all | solution.py:459
  504.3 2.7 copy.18
  507.0 3.6 reshape.470
  522.5 17.3 %kick_bricks.1 = f32[128,160,128]{2,1,0:T(8,128)} custom-call(s32[64]{0:T(128)} %fusion.8.index_ref, f32[5,64,2,16,128]{4,3,2,1,0:T(8,128)} %bitcast.92, f32[3,64,2,16,128]{4,3,2,1,0:T(8,128)} %pad_maximum_fusion.1.gradient_ref), custom_call_target="tpu_custom_call" | custom-call | tf_op jit(solution)/shard_map/kick_bricks/pallas_call | solution.py:425
  539.7 5.2 all-to-all-start.5
  546.1 225.0 %all-to-all-done.5 = f32[128,160,128]{2,1,0:T(8,128)} async-done(((f32[128,160,128]{2,1,0:T(8,128)}), f32[128,160,128]{2,1,0:T(8,128)}, u32[]{:S(2)}, u32[]{:S(2)}) %all-to-all-start.5) | async-done | bytes 10485792 | tf_op jit(solution)/shard_map/all_to_all | solution.py:459
  771.0 13.9 %unpack_slots.1 = f32[5,128,4096]{2,1,0:T(8,128)} custom-call(s32[2]{0:T(128)} %pad_add_fusion.info_ref, f32[8,8,2,160,128]{4,3,2,1,0:T(8,128)} %bitcast.37.in_ref), custom_call_target="tpu_custom_call" | custom-call | tf_op jit(solution)/shard_map/unpack_slots/pallas_call | solution.py:281
  (82 shorter events, 38.2 us)
Async XLA Ops:
  0.0 10.2 %collective-permute-start.6 = (s32[1,1]{1,0:T(1,128)}, s32[1,1]{1,0:T(1,128)}, u32[]{:S(2)}, u32[]{:S(2)}) collective-permute-start(s32[1,1]{1,0:T(1,128)} %param.7), channel_id=1, source_target_pairs={{0,7},{1,0},{2,1},{3,2},{4,3},{5,4},{6,5},{7,6},{8,15},{9,8},{10,9... | collective-permute-start | bytes 20 | tf_op jit(solution)/shard_map/ppermute | solution.py:533
  6.0 6.1 collective-permute-start.5
  6.4 6.8 collective-permute-start.4
  6.4 6.8 collective-permute-start.3
  9.4 5.6 collective-permute-start.2
  10.2 6.4 collective-permute-start.1
  12.1 6.3 collective-permute-start
  43.7 230.8 %all-to-all-start = ((f32[128,160,128]{2,1,0:T(8,128)}), f32[128,160,128]{2,1,0:T(8,128)}, u32[]{:S(2)}, u32[]{:S(2)}) async-start(f32[128,160,128]{2,1,0:T(8,128)} %bitcast.87), calls=%async_computation | async-start | bytes 20971520 | tf_op jit(solution)/shard_map/all_to_all | solution.py:459
  286.9 33.1 %copy-start = (f32[5,64,2,16,128]{4,3,2,1,0:T(8,128)S(1)}, f32[5,64,2,16,128]{4,3,2,1,0:T(8,128)}, u32[]{:S(2)}) copy-start(f32[5,64,2,16,128]{4,3,2,1,0:T(8,128)} %gather_bricks.1) | copy-start | bytes 15728644
  288.1 7.2 collective-permute-start.8
  288.2 10.1 %collective-permute-start.7 = (f32[5,4,32,128]{3,2,1,0:T(8,128)S(1)}, f32[5,4,32,128]{3,2,1,0:T(8,128)S(1)}, u32[]{:S(2)}, u32[]{:S(2)}) collective-permute-start(f32[5,4,32,128]{3,2,1,0:T(8,128)S(1)} %get-tuple-element.9), channel_id=1, source_target_pairs={{0,8},{8,16},{16,24},{24,0},{1,9},{9,17},{17,25},{25,1},{2,10},{10... | collective-permute-start | bytes 983048 | tf_op jit(solution)/shard_map/ppermute | solution.py:50
  300.3 18.6 %collective-permute-start.10 = (f32[5,72,4,128]{3,2,1,0:T(4,128)S(1)}, f32[5,72,4,128]{3,2,1,0:T(4,128)S(1)}, u32[]{:S(2)}, u32[]{:S(2)}) collective-permute-start(f32[5,72,4,128]{3,2,1,0:T(4,128)S(1)} %get-tuple-element.8), channel_id=1, source_target_pairs={{2,0},{4,2},{6,4},{7,6},{5,7},{3,5},{1,3},{0,1},{10,8},{12,10},{14... | collective-permute-start | bytes 2211848 | tf_op jit(solution)/shard_map/ppermute | solution.py:53
  301.9 18.1 %collective-permute-start.9 = (f32[5,72,4,128]{3,2,1,0:T(4,128)S(1)}, f32[5,72,4,128]{3,2,1,0:T(4,128)S(1)}, u32[]{:S(2)}, u32[]{:S(2)}) collective-permute-start(f32[5,72,4,128]{3,2,1,0:T(4,128)S(1)} %get-tuple-element.7), channel_id=1, source_target_pairs={{0,2},{2,4},{4,6},{6,7},{7,5},{5,3},{3,1},{1,0},{8,10},{10,12},{12... | collective-permute-start | bytes 2211848 | tf_op jit(solution)/shard_map/ppermute | solution.py:50
  324.7 64.5 %copy-start.5 = (f32[128,128]{1,0:T(8,128)S(1)}, f32[128,128]{1,0:T(8,128)}, u32[]{:S(2)}) copy-start(f32[128,128]{1,0:T(8,128)} %constant.153.clone) | copy-start | bytes 196612
  390.6 35.1 %copy-start.4 = (f32[4,64,256]{2,1,0:T(8,128)S(1)}, f32[4,64,256]{2,1,0:T(8,128)}, u32[]{:S(2)}) copy-start(f32[4,64,256]{2,1,0:T(8,128)} %constant.165) | copy-start | bytes 786436
  396.9 28.8 %all-to-all-start.1 = ((f32[8,32,1024]{2,1,0:T(8,128)}), f32[8,32,1024]{2,1,0:T(8,128)S(1)}, u32[]{:S(2)}, u32[]{:S(2)}) async-start(f32[8,32,1024]{2,1,0:T(8,128)} %copy.17), calls=%async_computation.1 | async-start | bytes 2097152 | tf_op jit(solution)/shard_map/all_to_all | solution.py:459
  427.7 18.0 %all-to-all-start.2 = ((f32[4,64,1024]{2,1,0:T(8,128)}), f32[4,64,1024]{2,1,0:T(8,128)S(1)}, u32[]{:S(2)}, u32[]{:S(2)}) async-start(f32[4,64,1024]{2,1,0:T(8,128)} %fusion.33), calls=%async_computation.2 | async-start | bytes 2097152 | tf_op jit(solution)/shard_map/all_to_all | solution.py:459
  433.0 18.4 %copy-start.2 = (f32[256,256]{1,0:T(8,128)S(1)}, f32[256,256]{1,0:T(8,128)}, u32[]{:S(2)}) copy-start(f32[256,256]{1,0:T(8,128)} %constant.152.clone) | copy-start | bytes 786436
  446.2 5.2 copy-start.1
  454.3 20.4 %copy-start.3 = (f32[8,32,256]{2,1,0:T(8,128)S(1)}, f32[8,32,256]{2,1,0:T(8,128)}, u32[]{:S(2)}) copy-start(f32[8,32,256]{2,1,0:T(8,128)} %constant.163) | copy-start | bytes 786436
  513.3 4.4 collective-permute-start.12
  513.4 4.4 collective-permute-start.11
  515.1 3.9 collective-permute-start.14
  516.2 3.9 collective-permute-start.13
  539.7 231.3 %all-to-all-start.5 = ((f32[128,160,128]{2,1,0:T(8,128)}), f32[128,160,128]{2,1,0:T(8,128)}, u32[]{:S(2)}, u32[]{:S(2)}) async-start(f32[128,160,128]{2,1,0:T(8,128)} %kick_bricks.1), calls=%async_computation.5 | async-start | bytes 20971520 | tf_op jit(solution)/shard_map/all_to_all | solution.py:459

commit v4 on v2

--- a/solution.py
+++ b/solution.py
@@ -467,7 +467,9 @@
     table_y = jnp.concatenate(
         [table_y[block * block_y : (block + 1) * block_y] for block in block_of("col")]
     )
-    along = matmul(density.reshape(block_x * block_y, GZ), table_z)
+    along = lax.optimization_barrier(
+        matmul(density.reshape(block_x * block_y, GZ), table_z)
+    )
     packed = along.reshape(block_x, block_y, cols_count, cols_z).transpose(2, 1, 3, 0)
     mid = exchange(packed.reshape(GY, cols_z * block_x), "col")
     spectrum = exchange(matmul(table_y.T, mid), "row")

time: 784 us -> 775 us (0.989)
  matrix products: 19.6 us -> 7.79 us
    dot_general x6, matrix products: 19.6 us -> 7.79 us  [matmul(): return jnp.matmul(a, b, precision=lax.Precision.HIGHEST)]
where the time goes in v4:
time: 775 us; the launch traced here: 773 us
  waiting for transfers between devices  516 us (67%)
  Pallas kernels  122 us (16%)
  blocking collectives  58.6 us (8%)
  local copies, waits for them, and re-layouts  28.8 us (4%)
  starting transfers between devices  24 us (3%)
  other arithmetic  14.8 us (2%)
  matrix products  7.79 us (1%)
    all_to_all x4, waiting for transfers between devices, exchange(): return lax.all_to_all(packed, axis, split_axis=0, concat_axis=0, tiled=True)  486 us
    pallas_call x1, Pallas kernels, advance(): pl.pallas_call(step_kernel, out_shape=jax.ShapeDtypeStruct(out_shape, jnp...  63.2 us
    all_to_all x2, blocking collectives, exchange(): return lax.all_to_all(packed, axis, split_axis=0, concat_axis=0, tiled=True)  45.5 us
    ppermute x4, waiting for transfers between devices, edges(): lax.ppermute(lax.slice_in_dim(block, 0, width, axis=dim), axis, backward)  24.1 us
    all_to_all x4, starting transfers between devices, exchange(): return lax.all_to_all(packed, axis, split_axis=0, concat_axis=0, tiled=True)  17.6 us
    pallas_call x1, Pallas kernels, kick_bricks(): pl.pallas_call(kick_kernel, out_shape=jax.ShapeDtypeStruct((buffer_rows,...  17.3 us
  transfers between devices with their start and end apart: 12, of which 10 were waited for; matrix products, arithmetic and copies ran while one was open for 1% of the time, Pallas kernels for 0%

profile of v4, /device:TPU:0, one launch (start us, length us, event | category | flops | bytes accessed | tf_op | source)
XLA Modules:
  0.0 772.9 jit_solution(7101658526172705406)
XLA Ops:
  2.6 13.1 %all-reduce = s32[8]{0:T(128)S(1)} all-reduce(s32[8]{0:T(128)S(1)} %bitcast_dynamic-update-slice_fusion), channel_id=1, replica_groups=mesh['row'=4,'col'=8] {'col'}, use_global_device_ids=true, to_apply=%add | all-reduce | flops 8 | bytes 64 | tf_op jit(solution)/shard_map/reshape | solution.py:542
  17.1 14.8 %pack_slots.1 = f32[8,8,2,160,128]{4,3,2,1,0:T(8,128)} custom-call(s32[1]{0:T(128)} %bitcast.4.start_ref, f32[5,128,4096]{2,1,0:T(8,128)} %bitcast.97), custom_call_target="tpu_custom_call" | custom-call | tf_op jit(solution)/shard_map/pack_slots/pallas_call | solution.py:219
  31.9 5.2 all-to-all-start
  38.8 223.7 %all-to-all-done.refs_0_.refs_1_.refs_2_.refs_3_.refs_4_.refs_5_.refs_6_.refs_7_ = f32[128,160,128]{2,1,0:T(8,128)} async-done(((f32[128,160,128]{2,1,0:T(8,128)}), f32[128,160,128]{2,1,0:T(8,128)}, u32[]{:S(2)}, u32[]{:S(2)}) %all-to-all-start) | async-done | bytes 10485792 | tf_op jit(solution)/shard_map/all_to_all | solution.py:459
  262.5 12.4 %gather_bricks.1 = f32[5,64,2,16,128]{4,3,2,1,0:T(8,128)} custom-call(s32[64]{0:T(128)} %fusion.9.index_ref, f32[128,160,128]{2,1,0:T(8,128)} %all-to-all-done.refs_0_.refs_1_.refs_2_.refs_3_.refs_4_.refs_5_.refs_6_.refs_7_, f32[128,160,128]{2,1,0:T(8,128)} %all-to-all-done.refs_0_.refs_1_.refs_2_.refs_3_.refs_4_.refs_5_.refs_6_.refs_7_, ...), custom_call_target="tpu_custom_call" | custom-call | tf_op jit(solution)/shard_map/gather_bricks/pallas_call | solution.py:351
  276.7 6.6 collective-permute-done.1
  283.3 3.0 collective-permute-done
  286.3 2.0 pad_maximum_fusion.8
  290.4 16.5 %collective-permute-done.3 = f32[5,72,4,128]{3,2,1,0:T(4,128)S(1)} collective-permute-done((f32[5,72,4,128]{3,2,1,0:T(4,128)S(1)}, f32[5,72,4,128]{3,2,1,0:T(4,128)S(1)}, u32[]{:S(2)}, u32[]{:S(2)}) %collective-permute-start.3) | collective-permute-done | bytes 737312 | tf_op jit(solution)/shard_map/ppermute | solution.py:53
  308.0 4.7 pad_maximum_fusion.ext_ref
  312.8 63.2 %gas_step.1 = f32[5,64,32,128]{3,2,1,0:T(8,128)} custom-call(f32[5,72,40,128]{3,2,1,0:T(8,128)} %pad_maximum_fusion.ext_ref), custom_call_target="tpu_custom_call" | custom-call | flops 331776000 | bytes 14745600 | tf_op jit(solution)/shard_map/gas_step/pallas_call | solution.py:163
  378.6 2.7 reshape.334
  381.3 3.6 copy.17
  384.9 3.6 all-to-all-start.1
  388.7 24.9 %all-to-all-done.1 = f32[8,32,1024]{2,1,0:T(8,128)S(1)} async-done(((f32[8,32,1024]{2,1,0:T(8,128)}), f32[8,32,1024]{2,1,0:T(8,128)S(1)}, u32[]{:S(2)}, u32[]{:S(2)}) %all-to-all-start.1) | async-done | bytes 1048608 | tf_op jit(solution)/shard_map/all_to_all | solution.py:459
  413.7 2.0 fusion.20
  415.7 3.7 all-to-all-start.2
  421.0 12.6 %all-to-all-done.2 = f32[4,64,1024]{2,1,0:T(8,128)S(1)} async-done(((f32[4,64,1024]{2,1,0:T(8,128)}), f32[4,64,1024]{2,1,0:T(8,128)S(1)}, u32[]{:S(2)}, u32[]{:S(2)}) %all-to-all-start.2) | async-done | bytes 1048608 | tf_op jit(solution)/shard_map/all_to_all | solution.py:459
  434.2 2.7 copy.22
  436.9 2.5 reshape.336
  443.8 2.0 all_to_all.35
  445.8 16.9 %all_to_all.46 = f32[4,64,1024]{2,1,0:T(8,128)S(1)} all-to-all(f32[4,64,1024]{2,1,0:T(8,128)S(1)} %all_to_all.35), channel_id=1, replica_groups=mesh['row'=4,'col'=8] {'row'}, dimensions={0} | all-to-all | bytes 2097152 | tf_op jit(solution)/shard_map/all_to_all | solution.py:459
  463.7 28.6 %all_to_all.47 = f32[8,32,1024]{2,1,0:T(8,128)S(1)} all-to-all(f32[8,32,1024]{2,1,0:T(8,128)S(1)} %fusion.22), channel_id=1, replica_groups=mesh['row'=4,'col'=8] {'col'}, dimensions={0} | all-to-all | bytes 2097152 | tf_op jit(solution)/shard_map/all_to_all | solution.py:459
  492.3 2.7 copy.18
  495.0 3.6 reshape.339
  498.7 1.8 fusion.23
  501.4 1.7 collective-permute-start.4
  508.4 2.0 pad_maximum_fusion.1.gradient_ref
  510.4 17.3 %kick_bricks.1 = f32[128,160,128]{2,1,0:T(8,128)} custom-call(s32[64]{0:T(128)} %fusion.9.index_ref, f32[5,64,2,16,128]{4,3,2,1,0:T(8,128)} %bitcast.94, f32[3,64,2,16,128]{4,3,2,1,0:T(8,128)} %pad_maximum_fusion.1.gradient_ref), custom_call_target="tpu_custom_call" | custom-call | tf_op jit(solution)/shard_map/kick_bricks/pallas_call | solution.py:425
  527.7 5.2 all-to-all-start.5
  534.0 225.0 %all-to-all-done.5 = f32[128,160,128]{2,1,0:T(8,128)} async-done(((f32[128,160,128]{2,1,0:T(8,128)}), f32[128,160,128]{2,1,0:T(8,128)}, u32[]{:S(2)}, u32[]{:S(2)}) %all-to-all-start.5) | async-done | bytes 10485792 | tf_op jit(solution)/shard_map/all_to_all | solution.py:459
  759.0 13.9 %unpack_slots.1 = f32[5,128,4096]{2,1,0:T(8,128)} custom-call(s32[2]{0:T(128)} %pad_add_fusion.info_ref, f32[8,8,2,160,128]{4,3,2,1,0:T(8,128)} %bitcast.34.in_ref), custom_call_target="tpu_custom_call" | custom-call | tf_op jit(solution)/shard_map/unpack_slots/pallas_call | solution.py:281
  (72 shorter events, 27.2 us)
Async XLA Ops:
  31.9 230.6 %all-to-all-start = ((f32[128,160,128]{2,1,0:T(8,128)}), f32[128,160,128]{2,1,0:T(8,128)}, u32[]{:S(2)}, u32[]{:S(2)}) async-start(f32[128,160,128]{2,1,0:T(8,128)} %bitcast.89), calls=%async_computation | async-start | bytes 20971520 | tf_op jit(solution)/shard_map/all_to_all | solution.py:459
  274.9 33.1 %copy-start = (f32[5,64,2,16,128]{4,3,2,1,0:T(8,128)S(1)}, f32[5,64,2,16,128]{4,3,2,1,0:T(8,128)}, u32[]{:S(2)}) copy-start(f32[5,64,2,16,128]{4,3,2,1,0:T(8,128)} %gather_bricks.1) | copy-start | bytes 15728644
  276.2 7.2 collective-permute-start.1
  276.2 10.1 %collective-permute-start = (f32[5,4,32,128]{3,2,1,0:T(8,128)S(1)}, f32[5,4,32,128]{3,2,1,0:T(8,128)S(1)}, u32[]{:S(2)}, u32[]{:S(2)}) collective-permute-start(f32[5,4,32,128]{3,2,1,0:T(8,128)S(1)} %get-tuple-element.7), channel_id=1, source_target_pairs={{0,8},{8,16},{16,24},{24,0},{1,9},{9,17},{17,25},{25,1},{2,10},{10... | collective-permute-start | bytes 983048 | tf_op jit(solution)/shard_map/ppermute | solution.py:50
  288.3 18.6 %collective-permute-start.3 = (f32[5,72,4,128]{3,2,1,0:T(4,128)S(1)}, f32[5,72,4,128]{3,2,1,0:T(4,128)S(1)}, u32[]{:S(2)}, u32[]{:S(2)}) collective-permute-start(f32[5,72,4,128]{3,2,1,0:T(4,128)S(1)} %get-tuple-element.6), channel_id=1, source_target_pairs={{2,0},{4,2},{6,4},{7,6},{5,7},{3,5},{1,3},{0,1},{10,8},{12,10},{14... | collective-permute-start | bytes 2211848 | tf_op jit(solution)/shard_map/ppermute | solution.py:53
  289.9 18.1 %collective-permute-start.2 = (f32[5,72,4,128]{3,2,1,0:T(4,128)S(1)}, f32[5,72,4,128]{3,2,1,0:T(4,128)S(1)}, u32[]{:S(2)}, u32[]{:S(2)}) collective-permute-start(f32[5,72,4,128]{3,2,1,0:T(4,128)S(1)} %get-tuple-element.5), channel_id=1, source_target_pairs={{0,2},{2,4},{4,6},{6,7},{7,5},{5,3},{3,1},{1,0},{8,10},{10,12},{12... | collective-permute-start | bytes 2211848 | tf_op jit(solution)/shard_map/ppermute | solution.py:50
  312.8 64.5 %copy-start.5 = (f32[128,128]{1,0:T(8,128)S(1)}, f32[128,128]{1,0:T(8,128)}, u32[]{:S(2)}) copy-start(f32[128,128]{1,0:T(8,128)} %constant.95.clone) | copy-start | bytes 196612
  378.6 35.1 %copy-start.4 = (f32[4,64,256]{2,1,0:T(8,128)S(1)}, f32[4,64,256]{2,1,0:T(8,128)}, u32[]{:S(2)}) copy-start(f32[4,64,256]{2,1,0:T(8,128)} %constant.107) | copy-start | bytes 786436
  384.9 28.7 %all-to-all-start.1 = ((f32[8,32,1024]{2,1,0:T(8,128)}), f32[8,32,1024]{2,1,0:T(8,128)S(1)}, u32[]{:S(2)}, u32[]{:S(2)}) async-start(f32[8,32,1024]{2,1,0:T(8,128)} %copy.17), calls=%async_computation.1 | async-start | bytes 2097152 | tf_op jit(solution)/shard_map/all_to_all | solution.py:459
  415.7 18.0 %all-to-all-start.2 = ((f32[4,64,1024]{2,1,0:T(8,128)}), f32[4,64,1024]{2,1,0:T(8,128)S(1)}, u32[]{:S(2)}, u32[]{:S(2)}) async-start(f32[4,64,1024]{2,1,0:T(8,128)} %fusion.20), calls=%async_computation.2 | async-start | bytes 2097152 | tf_op jit(solution)/shard_map/all_to_all | solution.py:459
  421.0 18.4 %copy-start.2 = (f32[256,256]{1,0:T(8,128)S(1)}, f32[256,256]{1,0:T(8,128)}, u32[]{:S(2)}) copy-start(f32[256,256]{1,0:T(8,128)} %constant.94.clone) | copy-start | bytes 786436
  434.2 5.2 copy-start.1
  442.2 20.4 %copy-start.3 = (f32[8,32,256]{2,1,0:T(8,128)S(1)}, f32[8,32,256]{2,1,0:T(8,128)}, u32[]{:S(2)}) copy-start(f32[8,32,256]{2,1,0:T(8,128)} %constant.105) | copy-start | bytes 786436
  501.3 4.4 collective-permute-start.5
  501.4 4.4 collective-permute-start.4
  503.1 3.9 collective-permute-start.7
  504.2 3.9 collective-permute-start.6
  527.7 231.3 %all-to-all-start.5 = ((f32[128,160,128]{2,1,0:T(8,128)}), f32[128,160,128]{2,1,0:T(8,128)}, u32[]{:S(2)}, u32[]{:S(2)}) async-start(f32[128,160,128]{2,1,0:T(8,128)} %kick_bricks.1), calls=%async_computation.5 | async-start | bytes 20971520 | tf_op jit(solution)/shard_map/all_to_all | solution.py:459
